TPU v7x, 256 devices: a whole 4x4x8 slice. The times are simulated.
256 devices in a mesh: dp: 8 (over y, x_hi), ctx: 32 (over x_lo, z, core).
Axes of the slice: x: 4 (x_hi: 2, x_lo: 2; x = x_hi * 2 + x_lo), y: 4, z: 8, core: 2. Of those that a mesh axis runs over, the one named last changes fastest.
Arguments:
- lengths: int32 [8], replicated, may hold values from 1024 to 4096, as said below
- query_states: bfloat16 [8, 4096, 512], P('dp', 'ctx'), may hold values from -60 to 60
- key_states: bfloat16 [8, 4096, 512], P('dp', 'ctx'), may hold values from -5.6 to 5.6
- value_states: bfloat16 [8, 4096, 512], P('dp', 'ctx'), may hold values from -24 to 24
- grad_output: bfloat16 [8, 4096, 512], P('dp', 'ctx'), may hold values from -6 to 6
- conv_kernel: float32 [31, 512], replicated, may hold values from -1 to 1
Outputs:
- mixed_out: bfloat16 [8, 4096, 512], P('dp', 'ctx')
- query_grad: bfloat16 [8, 4096, 512], P('dp', 'ctx')
- key_grad: bfloat16 [8, 4096, 512], P('dp', 'ctx')
- value_grad: bfloat16 [8, 4096, 512], P('dp', 'ctx')
- kernel_grad: float32 [31, 512], replicated
Inputs may be any that keep to these rules, and one draw needn't show every extreme that they name: `lengths`: one recording has all 4096 frames live.
All inputs are finite; a program needn't handle non-finite values.
Results may differ from a plain program's by a relative error of at most 0.04.
Values may be sent and summed in bfloat16 or wider, within the bound.
A program may use at most 128 MiB of HBM per device.

v0:
```python
import jax
import jax.numpy as jnp
from jax import lax
from jax.sharding import PartitionSpec as P

HEADS = 8
HEAD_DIM = 64


MASK_FILL = -1e30


def extended(block, sides, width):
    for axis, dim in sides:
        count = lax.axis_size(axis)
        forward = [(i, i + 1) for i in range(count - 1)]
        backward = [(target, source) for source, target in forward]
        low = lax.ppermute(
            lax.slice_in_dim(block, block.shape[dim] - width, None, axis=dim), axis, forward
        )
        high = lax.ppermute(lax.slice_in_dim(block, 0, width, axis=dim), axis, backward)
        block = jnp.concatenate([low, block, high], axis=dim)
    return block


def split_heads(tile):
    return tile.reshape(tile.shape[-2], HEADS, HEAD_DIM)


def spread(per_head):
    return jnp.repeat(per_head.T, HEAD_DIM, axis=1)


def tile_terms(query_rows, grad_rows, lse_rows, delta_rows, key_rows, value_rows, valid_keys):
    score_scale = HEAD_DIM ** (-0.5)
    scores = (
        jnp.einsum("qhd,khd->hqk", query_rows, key_rows, preferred_element_type=jnp.float32)
        * score_scale
    )
    probs = jnp.where(valid_keys[None, None, :], jnp.exp(scores - lse_rows[:, :, None]), 0.0)
    prob_grad = jnp.einsum(
        "qhd,khd->hqk", grad_rows, value_rows, preferred_element_type=jnp.float32
    )
    score_grad = (probs * (prob_grad - delta_rows[:, :, None])).astype(jnp.bfloat16)
    return (probs.astype(jnp.bfloat16), score_grad)


def per_device(lengths, query_states, key_states, value_states, grad_output, conv_kernel):
    shard_rows = query_states.shape[1]
    feature_width = query_states.shape[2]
    score_scale = HEAD_DIM ** (-0.5)
    half_width = (conv_kernel.shape[0] - 1) // 2
    record = lax.axis_index("dp")
    chosen = jnp.arange(lengths.shape[0], dtype=jnp.int32) == record
    length = jnp.sum(jnp.where(chosen, lengths, 0))
    first_row = lax.axis_index("ctx") * shard_rows
    positions = first_row + jnp.arange(shard_rows, dtype=jnp.int32)
    live_rows = positions < length
    live_column = live_rows.astype(jnp.float32)[:, None]
    local_query = split_heads(query_states[0])
    local_keys = split_heads(key_states[0])
    local_values = split_heads(value_states[0])
    pieces = (
        lax.all_gather(key_states, "ctx", axis=1, tiled=True),
        lax.all_gather(value_states, "ctx", axis=1, tiled=True),
    )
    key_rows = split_heads(pieces[0][0])
    value_rows = split_heads(pieces[1][0])
    valid_keys = jnp.arange(key_rows.shape[0], dtype=jnp.int32) < length
    running_max = jnp.full((HEADS, shard_rows), MASK_FILL, jnp.float32)
    weighted = jnp.zeros((shard_rows, feature_width), jnp.float32)
    scores = (
        jnp.einsum("qhd,khd->hqk", local_query, key_rows, preferred_element_type=jnp.float32)
        * score_scale
    )
    scores = jnp.where(valid_keys[None, None, :], scores, MASK_FILL)
    new_max = jnp.maximum(running_max, jnp.max(scores, axis=2))
    weights = jnp.where(valid_keys[None, None, :], jnp.exp(scores - new_max[:, :, None]), 0.0)
    factor = jnp.exp(running_max - new_max)
    update = jnp.einsum(
        "hqk,khd->qhd", weights.astype(jnp.bfloat16), value_rows, preferred_element_type=jnp.float32
    )
    update = update.reshape(shard_rows, feature_width)
    folded = (new_max, jnp.sum(weights, axis=2), weighted * spread(factor) + update)
    running_max, denominator, weighted = folded
    attention = (weighted / spread(denominator)).astype(jnp.bfloat16)
    lse_rows = running_max + jnp.log(denominator)
    attention_live = (attention.astype(jnp.float32) * live_column).astype(jnp.bfloat16)
    attention_rim = extended(attention_live, (("ctx", 0),), half_width).astype(jnp.float32)
    grad_live = (grad_output[0].astype(jnp.float32) * live_column).astype(jnp.bfloat16)
    grad_rim = extended(grad_live, (("ctx", 0),), half_width).astype(jnp.float32)
    grad_center = grad_rim[half_width : half_width + shard_rows]
    conv_out = jnp.zeros((shard_rows, feature_width), jnp.float32)
    conv_back = jnp.zeros((shard_rows, feature_width), jnp.float32)
    kernel_terms = []
    for tap in range(conv_kernel.shape[0]):
        window = attention_rim[tap : tap + shard_rows]
        conv_out = conv_out + conv_kernel[tap] * window
        back_begin = 2 * half_width - tap
        conv_back = conv_back + conv_kernel[tap] * grad_rim[back_begin : back_begin + shard_rows]
        kernel_terms.append(jnp.sum(grad_center * window, axis=0))
    kernel_grad = lax.psum(jnp.stack(kernel_terms), ("dp", "ctx"))
    mixed_out = ((attention_live.astype(jnp.float32) + conv_out) * live_column).astype(jnp.bfloat16)
    out_grad = ((grad_live.astype(jnp.float32) + conv_back) * live_column).astype(jnp.bfloat16)
    delta_rows = jnp.sum(
        (out_grad.astype(jnp.float32) * attention.astype(jnp.float32)).reshape(
            shard_rows, HEADS, HEAD_DIM
        ),
        axis=2,
    ).T
    all_lse, all_delta = (
        lax.all_gather(lse_rows, "ctx", axis=1, tiled=True),
        lax.all_gather(delta_rows, "ctx", axis=1, tiled=True),
    )
    grad_heads = split_heads(out_grad)
    out_grad_tile = out_grad[None]
    pieces = (
        lax.all_gather(key_states, "ctx", axis=1, tiled=True),
        lax.all_gather(value_states, "ctx", axis=1, tiled=True),
    )
    key_rows = split_heads(pieces[0][0])
    value_rows = split_heads(pieces[1][0])
    valid_keys = jnp.arange(key_rows.shape[0], dtype=jnp.int32) < length
    probs, score_grad = tile_terms(
        local_query, grad_heads, lse_rows, delta_rows, key_rows, value_rows, valid_keys
    )
    part = jnp.einsum("hqk,khd->qhd", score_grad, key_rows, preferred_element_type=jnp.float32)
    query_sum = part.reshape(shard_rows, feature_width)
    pieces = (
        lax.all_gather(query_states, "ctx", axis=1, tiled=True),
        lax.all_gather(out_grad_tile, "ctx", axis=1, tiled=True),
    )
    query_rows = split_heads(pieces[0][0])
    grad_rows = split_heads(pieces[1][0])
    probs, score_grad = tile_terms(
        query_rows, grad_rows, all_lse, all_delta, local_keys, local_values, live_rows
    )
    key_part = jnp.einsum(
        "hqk,qhd->khd", score_grad, query_rows, preferred_element_type=jnp.float32
    )
    value_part = jnp.einsum("hqk,qhd->khd", probs, grad_rows, preferred_element_type=jnp.float32)
    key_part, value_part = (
        key_part.reshape(shard_rows, feature_width),
        value_part.reshape(shard_rows, feature_width),
    )
    query_grad = (score_scale * query_sum).astype(jnp.bfloat16)[None]
    key_grad = (score_scale * key_part).astype(jnp.bfloat16)[None]
    value_grad = value_part.astype(jnp.bfloat16)[None]
    return (mixed_out[None], query_grad, key_grad, value_grad, kernel_grad)


def solution(mesh):
    placed = (
        P(),
        P("dp", "ctx", None),
        P("dp", "ctx", None),
        P("dp", "ctx", None),
        P("dp", "ctx", None),
        P(),
    )
    return jax.shard_map(
        per_device,
        mesh=mesh,
        in_specs=placed,
        out_specs=(
            P("dp", "ctx", None),
            P("dp", "ctx", None),
            P("dp", "ctx", None),
            P("dp", "ctx", None),
            P(),
        ),
        check_vma=False,
    )
```

profile of v0, /device:TPU:1, one launch (start us, length us, event | category | flops | bytes accessed | tf_op | source)
XLA Modules:
  0.0 435.1 jit_solution(15016872183630844506)
XLA Ops:
  7.2 0.0 all-gather.8.cloned.1.call-start
  7.2 0.7 all-gather.8.cloned.1.call-update
  7.9 0.0 all-gather.6.cloned.1.call-start
  7.9 0.7 all-gather.6.cloned.1.call-update
  8.7 0.0 all-gather.10.cloned.1.call-start
  8.7 0.7 all-gather.10.cloned.1.call-update
  9.4 0.0 all-gather.12.cloned.1.call-start
  9.4 1.0 copy.22
  10.5 1.0 copy.25
  11.5 1.3 fusion.66
  12.8 0.7 fusion.77
  13.5 0.7 iota_compare_fusion
  14.1 1.1 fusion.80
  15.3 65.6 %all-gather.8.cloned.1.call-done = bf16[1,4096,512]{2,1,0:T(8,128)(2,1)} async-done(((bf16[1,128,512]{2,1,0:T(8,128)(2,1)}), bf16[1,4096,512]{2,1,0:T(8,128)(2,1)}) %all-gather.8.cloned.1.call-update) | async-done | bytes 4194320 | tf_op jit(solution)/shard_map/all_gather | solution.py:65
  80.9 6.4 %copy.24 = bf16[1,4096,512]{1,2,0:T(8,128)(2,1)} copy(bf16[1,4096,512]{2,1,0:T(8,128)(2,1)} %all-gather.8.cloned.1.call-done) | data formatting | bytes 8388608 | tf_op jit(solution)/shard_map/all_gather | solution.py:65
  87.3 61.9 %all-gather.6.cloned.1.call-done = bf16[1,4096,512]{2,1,0:T(8,128)(2,1)} async-done(((bf16[1,128,512]{2,1,0:T(8,128)(2,1)}), bf16[1,4096,512]{2,1,0:T(8,128)(2,1)}) %all-gather.6.cloned.1.call-update) | async-done | bytes 4194320 | tf_op jit(solution)/shard_map/all_gather | solution.py:64
  149.3 6.4 %copy.23 = bf16[1,4096,512]{1,2,0:T(8,128)(2,1)} copy(bf16[1,4096,512]{2,1,0:T(8,128)(2,1)} %all-gather.6.cloned.1.call-done) | data formatting | bytes 8388608 | tf_op jit(solution)/shard_map/all_gather | solution.py:64
  155.6 4.5 %select_reduce_fusion = (f32[8,128]{1,0:T(8,128)S(1)}, f32[8,128,4096]{2,1,0:T(8,128)S(1)}) fusion(pred[4096]{0:T(1024)(128)(4,1)S(1)} %iota_compare_fusion, bf16[128,8,64]{0,2,1:T(8,128)(2,1)S(1)} %bitcast.133, bf16[4096,8,64]{0,2,1:T(8,128)(2,1)} %bitcast.129), kind=kOutput, calls=%fused_computation.4 | convolution fusion | flops 549452800 | bytes 21110784 | tf_op jit(solution)/shard_map/qhd,khd->hqk/dot_general | solution.py:73
  160.1 0.0 copy-start
  160.1 5.7 %copy-done = f32[8,128,4096]{2,1,0:T(8,128)} copy-done((f32[8,128,4096]{2,1,0:T(8,128)}, f32[8,128,4096]{2,1,0:T(8,128)S(1)}, u32[]{:S(2)}) %copy-start) | copy-done | bytes 16777240
  165.8 4.8 %fusion.1 = f32[8,128]{1,0:T(8,128)S(1)} fusion(f32[8,128,4096]{2,1,0:T(8,128)S(1)} %get-tuple-element.94, f32[8,128]{1,0:T(8,128)S(1)} %broadcast_maximum_fusion, pred[4096]{0:T(1024)(128)(4,1)S(1)} %iota_compare_fusion), kind=kLoop, calls=%fused_computation.6 | loop fusion | flops 20970496 | bytes 16789504 | tf_op jit(solution)/shard_map/reduce_sum | solution.py:84
  170.7 0.0 copy-start.3
  170.7 0.0 copy-start.4
  170.7 11.4 %fusion.27 = bf16[128,8,64]{0,2,1:T(8,128)(2,1)S(1)} fusion(bf16[4096,8,64]{0,2,1:T(8,128)(2,1)} %bitcast.131, f32[8,128,4096]{2,1,0:T(8,128)} %copy-done, f32[8,128]{1,0:T(8,128)S(1)} %broadcast_maximum_fusion, pred[4096]{0:T(1024)(128)(4,1)S(1)} %iota_compare_fusion, f32[128,8]{0,1:T(8,128)S(1)} %bitcast.204, f32[128,8]{0,1:T(8,128)S(1)} %get-tuple-element.90), kind=kOutput, calls=%fused_computation.22 | convolution fusion | flops 558039040 | bytes 21118976 | tf_op jit(solution)/shard_map/hqk,khd->qhd/dot_general | solution.py:80
  182.1 0.1 fusion.64
  182.2 0.1 fusion.78
  182.3 2.1 collective-permute-start.3
  184.4 3.4 collective-permute-start.2
  187.9 1.0 fusion.81
  188.9 1.0 collective-permute-done.3
  189.9 1.3 collective-permute-done.2
  191.3 0.2 maximum_convert_fusion.1
  191.4 5.2 %bitcast_reduce_fusion = (f32[128,8]{0,1:T(8,128)S(1)}, bf16[128,512]{0,1:T(8,128)(2,1)}) fusion(bf16[128,8,64]{0,2,1:T(8,128)(2,1)S(1)} %fusion.27, f32[158,512]{0,1:T(8,128)S(1)} %maximum_convert_fusion.1, f32[512]{0:T(512)S(1)} %bitcast.198, f32[512]{0:T(512)S(1)} %bitcast.200, f32[512]{0:T(512)S(1)} %bitcast.142, f32[512]{0:T(512)S(1)} %bitcast.144, ...), kind=kLoop, calls=%fused_computation.93 | loop fusion | flops 4717568 | bytes 8587776 | tf_op jit(solution)/shard_map/reduce_sum | solution.py:105
  196.7 0.0 all-gather.12.cloned.1.call-update
  196.7 0.1 copy.27
  196.8 0.1 copy.28
  197.0 0.1 fusion.79
  197.1 1.9 collective-permute-start.1
  199.0 4.5 %collective-permute-start = (bf16[15,512]{0,1:T(8,128)(2,1)S(1)}, bf16[15,512]{0,1:T(8,128)(2,1)S(1)}, u32[]{:S(2)}, u32[]{:S(2)}) collective-permute-start(bf16[15,512]{0,1:T(8,128)(2,1)S(1)} %get-tuple-element.56), channel_id=1, source_target_pairs={{0,1},{1,2},{2,3},{3,4},{4,5},{5,6},{6,7},{7,8},{8,9},{9,10},{10,1... | collective-permute-start | bytes 46088 | tf_op jit(solution)/shard_map/ppermute | solution.py:18
  203.5 14.6 %all-gather.10.cloned.1.call-done = bf16[1,4096,512]{2,1,0:T(8,128)(2,1)} async-done(((bf16[1,128,512]{2,1,0:T(8,128)(2,1)}), bf16[1,4096,512]{2,1,0:T(8,128)(2,1)}) %all-gather.10.cloned.1.call-update) | async-done | bytes 4194320 | tf_op jit(solution)/shard_map/all_gather | solution.py:130
  218.1 6.4 %copy.26 = bf16[1,4096,512]{1,2,0:T(8,128)(2,1)} copy(bf16[1,4096,512]{2,1,0:T(8,128)(2,1)} %all-gather.10.cloned.1.call-done) | data formatting | bytes 8388608 | tf_op jit(solution)/shard_map/all_gather | solution.py:130
  224.5 10.6 %fusion.82 = f32[8,4096,128]{2,1,0:T(8,128)} fusion(bf16[4096,8,64]{0,2,1:T(8,128)(2,1)} %bitcast.127, bf16[128,8,64]{0,2,1:T(8,128)(2,1)S(1)} %bitcast.136), kind=kOutput, calls=%fused_computation.148 | convolution fusion | flops 536870912 | bytes 21102592 | tf_op jit(solution)/shard_map/qhd,khd->hqk/dot_general | solution.py:37
  235.1 33.0 %all_gather.23 = f32[8,4096]{1,0:T(8,128)S(1)} all-gather(f32[8,128]{1,0:T(8,128)S(1)} %get-tuple-element.89), channel_id=1, replica_groups=mesh['dp'=8,'ctx'=32] {'ctx'}, dimensions={1}, use_global_device_ids=true | all-gather | bytes 135168 | tf_op jit(solution)/shard_map/all_gather | solution.py:112
  268.1 0.0 collective-permute-done.1
  268.1 0.0 collective-permute-done
  268.1 0.2 maximum_convert_fusion
  268.3 4.6 %fusion.65 = bf16[1,128,512]{1,2,0:T(8,128)(2,1)S(1)} fusion(f32[128]{0:T(128)S(1)} %get-tuple-element.48, f32[158,512]{0,1:T(8,128)S(1)} %maximum_convert_fusion, f32[512]{0:T(512)S(1)} %bitcast.199, f32[512]{0:T(512)S(1)} %bitcast.201, f32[512]{0:T(512)S(1)} %bitcast.143, f32[512]{0:T(512)S(1)} %bitcast.145, f32[512]{0:T(512)S(1)} %bitcast.147, ...), kind=kLoop, calls=%fused_computation.126 | loop fusion | flops 4456448 | bytes 8452608 | tf_op jit(solution)/shard_map/broadcast_in_dim | solution.py:149
  272.9 0.8 copy.29
  273.7 0.0 copy-done.2
  273.7 12.5 %fusion.20 = bf16[8,128,64]{1,2,0:T(8,128)(2,1)S(1)} fusion(bf16[4096,8,64]{0,2,1:T(8,128)(2,1)} %bitcast.130, f32[8,128,4096]{2,1,0:T(8,128)} %copy-done, bf16[128,8,64]{0,2,1:T(8,128)(2,1)S(1)} %bitcast.135, bf16[4096,8,64]{0,2,1:T(8,128)(2,1)} %bitcast.132, f32[8,128]{1,0:T(8,128)S(1)} %bitcast.202, f32[8,128]{1,0:T(8,128)S(1)} %get-tuple-element.89, ...), kind=kOutput, calls=%fused_computation.19 | convolution fusion | flops 1099038720 | bytes 25440256 | tf_op jit(solution)/shard_map/hqk,khd->qhd/dot_general | solution.py:127
  286.2 0.8 copy.30
  286.9 1.4 multiply_reduce_fusion.18
  288.3 1.4 multiply_reduce_fusion.9
  289.7 1.9 multiply_reduce_fusion
  291.6 0.2 stack.127
  291.8 75.4 %psum.7 = f32[31,512]{1,0:T(8,128)} all-reduce(f32[31,512]{1,0:T(8,128)S(1)} %stack.127), channel_id=1, replica_groups=mesh['dp'=8,'ctx'=32] {'dp','ctx'}, use_global_device_ids=true, to_apply=%region_35.36 | all-reduce | flops 15872 | bytes 126976 | tf_op jit(solution)/shard_map/psum | solution.py:102
  367.1 34.3 %all_gather.25 = f32[8,4096]{1,0:T(8,128)S(1)} all-gather(f32[8,128]{1,0:T(8,128)S(1)} %bitcast.203), channel_id=1, replica_groups=mesh['dp'=8,'ctx'=32] {'ctx'}, dimensions={1}, use_global_device_ids=true | all-gather | bytes 135168 | tf_op jit(solution)/shard_map/all_gather | solution.py:113
  401.4 9.9 %fusion.21 = bf16[8,64,128]{2,1,0:T(8,128)(2,1)S(1)} fusion(bf16[4096,8,64]{0,2,1:T(8,128)(2,1)} %bitcast.236, f32[8,4096,128]{2,1,0:T(8,128)} %fusion.82, f32[8,4096]{1,0:T(8,128)S(1)} %all_gather.23, pred[128]{0:T(512)(128)(4,1)S(1)} %get-tuple-element.49), kind=kOutput, calls=%fused_computation.20 | convolution fusion | flops 553713664 | bytes 21233792 | tf_op jit(solution)/shard_map/hqk,qhd->khd/dot_general | solution.py:141
  411.3 0.0 copy-done.5
  411.4 0.0 copy-start.1
  411.4 14.1 %multiply_convert_fusion.clone.8 = bf16[8,4096,128]{2,1,0:T(8,128)(2,1)S(1)} fusion(f32[8,4096,128]{2,1,0:T(8,128)} %fusion.82, bf16[4096,8,64]{0,2,1:T(8,128)(2,1)S(1)} %bitcast.237, bf16[128,8,64]{0,2,1:T(8,128)(2,1)S(1)} %bitcast.137, f32[8,4096]{1,0:T(8,128)S(1)} %all_gather.25, f32[8,4096]{1,0:T(8,128)S(1)} %all_gather.23, ...), kind=kOutput, calls=%fused_computation.clone.clone.clone.clone.clone.clone.clone.1 | convolution fusion | flops 562036736 | bytes 29753472 | tf_op jit(solution)/shard_map/qhd,khd->hqk/dot_general | solution.py:41
  425.5 1.6 fusion.19
  427.1 0.8 copy.31
  427.8 0.8 copy.32
  (8 shorter events, 0.0 us)
Async XLA Ops:
  7.2 73.7 %all-gather.8.cloned.1.call-start = ((), (), s32[]{:S(2)}) async-start(), calls=%async_computation.1 | async-start | bytes 4325376 | tf_op jit(solution)/shard_map/all_gather | solution.py:65
  7.9 141.4 %all-gather.6.cloned.1.call-start = ((), (), s32[]{:S(2)}) async-start(), calls=%async_computation | async-start | bytes 4325376 | tf_op jit(solution)/shard_map/all_gather | solution.py:64
  8.7 209.5 %all-gather.10.cloned.1.call-start = ((), (), s32[]{:S(2)}) async-start(), calls=%async_computation.2 | async-start | bytes 4325376 | tf_op jit(solution)/shard_map/all_gather | solution.py:130
  9.4 392.1 %all-gather.12.cloned.1.call-start = ((), (), s32[]{:S(2)}) async-start(), calls=%async_computation.3 | async-start | bytes 4325376 | tf_op jit(solution)/shard_map/all_gather | solution.py:131
  160.1 5.7 %copy-start = (f32[8,128,4096]{2,1,0:T(8,128)}, f32[8,128,4096]{2,1,0:T(8,128)S(1)}, u32[]{:S(2)}) copy-start(f32[8,128,4096]{2,1,0:T(8,128)S(1)} %get-tuple-element.94) | copy-start | bytes 50331652
  170.7 26.0 %copy-start.3 = (bf16[1,128,512]{2,1,0:T(8,128)(2,1)S(1)}, bf16[1,128,512]{2,1,0:T(8,128)(2,1)}, u32[]{:S(2)}) copy-start(bf16[1,128,512]{2,1,0:T(8,128)(2,1)} %param.8) | copy-start | bytes 393220
  170.7 26.1 %copy-start.4 = (bf16[1,128,512]{2,1,0:T(8,128)(2,1)S(1)}, bf16[1,128,512]{2,1,0:T(8,128)(2,1)}, u32[]{:S(2)}) copy-start(bf16[1,128,512]{2,1,0:T(8,128)(2,1)} %param.9) | copy-start | bytes 393220
  182.3 7.6 %collective-permute-start.3 = (bf16[15,512]{0,1:T(8,128)(2,1)S(1)}, bf16[15,512]{0,1:T(8,128)(2,1)S(1)}, u32[]{:S(2)}, u32[]{:S(2)}) collective-permute-start(bf16[15,512]{0,1:T(8,128)(2,1)S(1)} %get-tuple-element.55), channel_id=1, source_target_pairs={{1,0},{2,1},{3,2},{4,3},{5,4},{6,5},{7,6},{8,7},{9,8},{10,9},{11,1... | collective-permute-start | bytes 46088 | tf_op jit(solution)/shard_map/ppermute | solution.py:21
  184.4 6.8 %collective-permute-start.2 = (bf16[15,512]{0,1:T(8,128)(2,1)S(1)}, bf16[15,512]{0,1:T(8,128)(2,1)S(1)}, u32[]{:S(2)}, u32[]{:S(2)}) collective-permute-start(bf16[15,512]{0,1:T(8,128)(2,1)S(1)} %get-tuple-element.54), channel_id=1, source_target_pairs={{0,1},{1,2},{2,3},{3,4},{4,5},{5,6},{6,7},{7,8},{8,9},{9,10},{10,1... | collective-permute-start | bytes 46088 | tf_op jit(solution)/shard_map/ppermute | solution.py:18
  197.1 71.0 %collective-permute-start.1 = (bf16[15,512]{0,1:T(8,128)(2,1)S(1)}, bf16[15,512]{0,1:T(8,128)(2,1)S(1)}, u32[]{:S(2)}, u32[]{:S(2)}) collective-permute-start(bf16[15,512]{0,1:T(8,128)(2,1)S(1)} %get-tuple-element.57), channel_id=1, source_target_pairs={{1,0},{2,1},{3,2},{4,3},{5,4},{6,5},{7,6},{8,7},{9,8},{10,9},{11,1... | collective-permute-start | bytes 46088 | tf_op jit(solution)/shard_map/ppermute | solution.py:21
  199.0 69.1 %collective-permute-start = (bf16[15,512]{0,1:T(8,128)(2,1)S(1)}, bf16[15,512]{0,1:T(8,128)(2,1)S(1)}, u32[]{:S(2)}, u32[]{:S(2)}) collective-permute-start(bf16[15,512]{0,1:T(8,128)(2,1)S(1)} %get-tuple-element.56), channel_id=1, source_target_pairs={{0,1},{1,2},{2,3},{3,4},{4,5},{5,6},{6,7},{7,8},{8,9},{9,10},{10,1... | collective-permute-start | bytes 46088 | tf_op jit(solution)/shard_map/ppermute | solution.py:18
  224.5 49.2 %copy-start.2 = (bf16[128,512]{0,1:T(8,128)(2,1)S(1)}, bf16[128,512]{0,1:T(8,128)(2,1)}, u32[]{:S(2)}) copy-start(bf16[128,512]{0,1:T(8,128)(2,1)} %get-tuple-element.47) | copy-start | bytes 393220
  401.4 9.9 %copy-start.5 = (bf16[4096,512]{0,1:T(8,128)(2,1)S(1)}, bf16[4096,512]{0,1:T(8,128)(2,1)}, u32[]{:S(2)}) copy-start(bf16[4096,512]{0,1:T(8,128)(2,1)} %all-gather.12.cloned.1.call-done) | copy-start | bytes 12582916
  411.4 14.1 %copy-start.1 = (bf16[1,4096,512]{1,2,0:T(8,128)(2,1)S(1)}, bf16[1,4096,512]{1,2,0:T(8,128)(2,1)}, u32[]{:S(2)}) copy-start(bf16[1,4096,512]{1,2,0:T(8,128)(2,1)} %copy.26) | copy-start | bytes 12582916
Sparse Core Ops, SparseCore 0:
  9.9 71.0 all-gather.7
  82.8 66.4 all-gather.5
  151.1 66.9 all-gather.9
  220.3 71.5 all-gather.11
where the time goes:
time: 436 us; the launch traced here: 435 us
  waiting for transfers between devices  147 us (34%)
  blocking collectives  143 us (33%)
  matrix products  64.5 us (15%)
  local copies, waits for them, and re-layouts  32.8 us (8%)
  other arithmetic  22.4 us (5%)
  between operations  14 us (3%)
  starting transfers between devices  12.1 us (3%)
    psum x1, blocking collectives, per_device(): kernel_grad = lax.psum(jnp.stack(kernel_terms), ('dp', 'ctx'))  75.4 us
    all_gather x1, waiting for transfers between devices, per_device(): lax.all_gather(value_states, 'ctx', axis=1, tiled=True)  65.6 us
    all_gather x1, waiting for transfers between devices, per_device(): lax.all_gather(key_states, 'ctx', axis=1, tiled=True)  61.9 us
    all_gather x1, blocking collectives, per_device(): lax.all_gather(delta_rows, 'ctx', axis=1, tiled=True)  34.3 us
    all_gather x1, blocking collectives, per_device(): lax.all_gather(lse_rows, 'ctx', axis=1, tiled=True)  33 us
    all_gather x1, waiting for transfers between devices, per_device(): lax.all_gather(query_states, 'ctx', axis=1, tiled=True)  14.6 us
    dot_general x1, matrix products, tile_terms(): jnp.einsum('qhd,khd->hqk', grad_rows, value_rows, preferred_element_type=...  14.1 us
    dot_general x1, matrix products, per_device(): jnp.einsum('hqk,khd->qhd', score_grad, key_rows, preferred_element_type=j...  12.5 us
  transfers between devices with their start and end apart: 8, of which 5 were waited for; matrix products, arithmetic and copies ran while one was open for 20% of the time, Pallas kernels for 0%

commit v1 on v0

v1 whole, which is shorter than its diff:
```python
import functools

import jax
import jax.numpy as jnp
from jax import lax
from jax.experimental import pallas as pl
from jax.experimental.pallas import tpu as pltpu
from jax.sharding import PartitionSpec as P

MESH = pl.DeviceIdType.MESH
D = 64
R = 128
FILL = -1e30
F32 = jnp.float32
BF16 = jnp.bfloat16

NN = (((1,), (0,)), ((), ()))
NT = (((1,), (1,)), ((), ()))


def dot(a, b, dims=NN):
    return lax.dot_general(a, b, dims, preferred_element_type=F32)


def kernel(
    Z, NDP, CK,
    len_ref, q_ref, k_ref, v_ref, g_ref, ck_ref,
    mix_out, dq_out, dk_out, dv_out, kg_out,
    snd_kv, snd_q, snd_g, kvt, kvn, kaug, qt, qaug, gseq, oseq, dot_t, gfc,
    kb, kga, kgt, kg_grp, kg_dp, kg_z, kg_s1, kg_s2,
    w_all, m_all, m_run, l_run, acc, dq_acc, mix_s, dq_s, part, gred, kv_s, rcv_m, rcv_q, rcv_kv,
    s_kv, r_kv, s_q, r_q, s_g, r_g, s_grp, r_grp, s_h, r_h,
    s_kg, r_kg, s_m, r_m, s_dq, r_dq, s_p, r_p, s_o, r_o,
):
    NQ = R * Z
    T = ck_ref.shape[0]
    HALF = (T - 1) // 2
    me = lax.axis_index("ctx")
    dp = lax.axis_index("dp")
    x = me // (2 * Z)
    z = (me // 2) % Z
    c = me % 2
    gm = 2 * x + c
    length = len_ref[dp]

    def zpeer(p):
        return (dp, x * 2 * Z + 2 * p + c)

    def gpeer(g):
        return (dp, (g // 2) * 2 * Z + 2 * z + g % 2)

    def rcopy(src, dst, ssem, rsem, dev):
        return pltpu.make_async_remote_copy(
            src_ref=src, dst_ref=dst, send_sem=ssem, recv_sem=rsem, device_id=dev, device_id_type=MESH
        )

    zorder = []
    for i in range(1, Z // 2 + 1):
        zorder.append(i)
        if Z - i != i:
            zorder.append(Z - i)

    zero_blk = jnp.zeros((D, R), BF16)
    for s in (gseq, oseq):
        s[0, 0] = zero_blk
        s[Z, 1] = zero_blk

    barrier = pltpu.get_barrier_semaphore()
    for i in range(1, Z):
        pl.semaphore_signal(barrier, inc=1, device_id=zpeer((z + i) % Z), device_id_type=MESH)
    for i in range(1, 4):
        pl.semaphore_signal(barrier, inc=1, device_id=gpeer((gm + i) % 4), device_id_type=MESH)
    for i in range(1, NDP):
        pl.semaphore_signal(barrier, inc=1, device_id=((dp + i) % NDP, me), device_id_type=MESH)

    my_frames = me * R + lax.broadcasted_iota(jnp.int32, (1, R), 1)
    my_live = (my_frames < length).astype(F32)
    turned = lambda ref: ref[...].astype(F32).T
    snd_q[...] = turned(q_ref).astype(BF16).reshape(Z, D, R)
    snd_kv[:, 0:D, :] = turned(k_ref).astype(BF16).reshape(Z, D, R)
    snd_kv[:, D : 2 * D, :] = turned(v_ref).astype(BF16).reshape(Z, D, R)
    snd_g[...] = (turned(g_ref) * my_live).astype(BF16).reshape(Z, D, R)

    pl.semaphore_wait(barrier, (Z - 1) + 3 + (NDP - 1))

    def cols(j):
        return pl.ds(pl.multiple_of(j * R, R), R)

    def seq_at(ref, p):
        return ref.at[p // 2, p % 2]

    sends = []
    for i in zorder:
        p = (z + i) % Z
        cp = rcopy(snd_kv.at[p], kvt.at[gm, :, cols(z)], s_kv.at[i], r_kv.at[z], zpeer(p))
        cp.start()
        sends.append(cp)
    for i in zorder:
        p = (z + i) % Z
        cp = rcopy(snd_q.at[p], qt.at[:, cols(z)], s_q.at[i], r_q.at[z], zpeer(p))
        cp.start()
        sends.append(cp)
    for i in zorder:
        p = (z + i) % Z
        cp = rcopy(snd_g.at[p], seq_at(gseq, 1 + 2 * z + c), s_g.at[i], r_g.at[z], zpeer(p))
        cp.start()
        sends.append(cp)
    kvt[gm, :, cols(z)] = snd_kv[z]
    qt[:, cols(z)] = snd_q[z]
    gseq[(1 + 2 * z + c) // 2, (1 + 2 * z + c) % 2] = snd_g[z]

    kgt[...] = jnp.zeros_like(kgt)
    kgt[0:T, :] = ck_ref[...]
    for b in range(Z * D // R):
        kg_s1[b * R : (b + 1) * R, :] = kgt[:, b * R : (b + 1) * R].T
    my_taps = kg_s1[pl.ds(pl.multiple_of(z * D, D), D), :]
    for t in range(T):
        kb[t] = jnp.broadcast_to(my_taps[:, t : t + 1], (D, R))

    for i in zorder:
        p = (z + i) % Z
        rcopy(snd_kv.at[p], kvt.at[gm, :, cols(p)], s_kv.at[i], r_kv.at[p], zpeer(p)).wait_recv()
    for i in range(1, 4):
        cp = rcopy(kvt.at[gm], kvt.at[gm], s_grp.at[i], r_grp.at[gm], gpeer((gm + i) % 4))
        cp.start()
        sends.append(cp)
    for i in zorder:
        p = (z + i) % Z
        rcopy(snd_q.at[p], qt.at[:, cols(p)], s_q.at[i], r_q.at[p], zpeer(p)).wait_recv()
    for i in zorder:
        p = (z + i) % Z
        rcopy(snd_g.at[p], seq_at(gseq, 1 + 2 * p + c), s_g.at[i], r_g.at[p], zpeer(p)).wait_recv()

    def halo(seq, n):
        mine = seq.at[pl.ds(c, Z), 1 - c]
        cp = rcopy(mine, mine, s_h.at[n], r_h.at[n], gpeer(gm + 1 - 2 * c))
        cp.start()

        @pl.when(x != c)
        def _():
            rcopy(
                seq.at[c * Z, 1 - c], seq.at[(1 - c) * Z, 1 - c],
                s_h.at[n + 1], r_h.at[n + 1], gpeer(3 - gm),
            ).start()

    def halo_wait(seq, n):
        mine = seq.at[pl.ds(c, Z), 1 - c]
        other = seq.at[pl.ds(1 - c, Z), c]
        cp = rcopy(mine, other, s_h.at[n], r_h.at[n], gpeer(gm + 1 - 2 * c))
        cp.wait_send()
        cp.wait_recv()

        @pl.when(x != c)
        def _():
            cp2 = rcopy(
                seq.at[c * Z, 1 - c], seq.at[c * Z, c],
                s_h.at[n + 1], r_h.at[n + 1], gpeer(3 - gm),
            )
            cp2.wait_send()
            cp2.wait_recv()

    halo(gseq, 0)
    qaug[0:D, :] = (qt[...].astype(F32) * (D ** -0.5)).astype(BF16)
    row = lax.broadcasted_iota(jnp.int32, (D, NQ), 0)
    qaug[D : 2 * D, :] = jnp.where(row == 0, 1.0, 0.0).astype(BF16)
    halo_wait(gseq, 0)

    lane = lax.broadcasted_iota(jnp.int32, (1, R), 1)

    def live_of(j):
        return ((x * 2 * Z + 2 * j + c) * R + lane < length).astype(F32)

    def window(seq, j):
        p = 1 + 2 * j + c
        parts = [seq[(p + d) // 2, (p + d) % 2].astype(F32) for d in (-1, 0, 1)]
        return jnp.concatenate(parts, axis=1), parts[1]

    def shifted(wide, s):
        if s == 0:
            return wide[:, R : 2 * R]
        return pltpu.roll(wide, (3 * R - s) % (3 * R), 1)[:, R : 2 * R]

    def grad_block(j, carry):
        wide, mid = window(gseq, j)
        total = mid
        for t in range(T):
            total = total + kb[t] * shifted(wide, HALF - t)
        dot_t[:, cols(j)] = (total * live_of(j)).astype(BF16)
        return carry

    lax.fori_loop(0, Z, grad_block, 0)

    for i in range(1, 4):
        g = (gm + i) % 4
        rcopy(kvt.at[g], kvt.at[g], s_grp.at[i], r_grp.at[g], gpeer(g)).wait_recv()

    lane_full = lax.broadcasted_iota(jnp.int32, (R, R), 1)
    sub_full = lax.broadcasted_iota(jnp.int32, (R, R), 0)

    def turn_block(n, carry):
        g = n // Z
        j = n % Z
        blk = kvt[g, :, cols(j)].astype(F32).T
        at = pl.ds(pl.multiple_of(n * R, R), R)
        kvn[at, :] = blk.astype(BF16)
        frame = ((g // 2) * 2 * Z + 2 * j + g % 2) * R + sub_full
        fill = jnp.where((lane_full == D) & (frame >= length), FILL, 0.0)
        kaug[at, :] = jnp.where(lane_full < D, blk, fill).astype(BF16)
        return carry

    lax.fori_loop(0, 4 * Z, turn_block, 0)

    m_run[...] = jnp.full(m_run.shape, FILL, F32)
    l_run[...] = jnp.zeros_like(l_run)
    acc[...] = jnp.zeros_like(acc)
    per_g = NQ // CK

    def forward(n, carry):
        at = pl.ds(pl.multiple_of(n * CK, CK), CK)
        s = dot(kaug[at, :], qaug[...])
        m_old = m_run[0:1, :]
        m_new = jnp.maximum(m_old, jnp.max(s, axis=0, keepdims=True))
        w = jnp.exp(s - m_new)
        alpha = jnp.exp(m_old - m_new)
        l_run[0:1, :] = l_run[0:1, :] * alpha + jnp.sum(w, axis=0, keepdims=True)
        wb = w.astype(BF16)
        w_all[at, :] = wb
        lanes = pl.ds(pl.multiple_of((n % per_g) * CK, CK), CK)
        acc[...] = acc[...] * alpha + dot(kvt[n // per_g, D : 2 * D, lanes], wb)
        m_run[0:1, :] = m_new
        m_all[n, 0:1, :] = m_new
        return carry

    lax.fori_loop(0, 4 * per_g, forward, 0)

    inv = 1.0 / l_run[0:1, :]
    l_run[0:1, :] = inv
    att = (acc[...] * inv).astype(BF16)
    for j in range(Z):
        blk = (att[:, j * R : (j + 1) * R].astype(F32) * live_of(j)).astype(BF16)
        oseq[(1 + 2 * j + c) // 2, (1 + 2 * j + c) % 2] = blk
    delta = jnp.sum(dot_t[...].astype(F32) * att.astype(F32), axis=0, keepdims=True)
    m_fin = m_run[0:1, :]
    halo(oseq, 2)
    kga[...] = jnp.zeros_like(kga)
    halo_wait(oseq, 2)

    def out_block(j, carry):
        wide, mid = window(oseq, j)
        p = 1 + 2 * j + c
        grad = gseq[p // 2, p % 2].astype(F32)
        total = mid
        for t in range(T):
            seg = shifted(wide, t - HALF)
            total = total + kb[t] * seg
            kga[t] = kga[t] + grad * seg
        mix_s[j] = (total * live_of(j)).astype(BF16)
        return carry

    lax.fori_loop(0, Z, out_block, 0)

    for i in zorder:
        p = (z + i) % Z
        cp = rcopy(mix_s.at[p], rcv_m.at[z], s_m.at[i], r_m.at[z], zpeer(p))
        cp.start()
        sends.append(cp)
    rcv_m[z] = mix_s[z]

    lane_d = lax.broadcasted_iota(jnp.int32, (D, R), 1)
    red = jnp.zeros((D, R), F32)
    for t in range(T):
        red = jnp.where(lane_d == t, jnp.sum(kga[t], axis=1, keepdims=True), red)
    kg_grp[gm] = jnp.concatenate([red, jnp.zeros((R - D, R), F32)], axis=0).T[0:32, :]
    for i in range(1, 4):
        cp = rcopy(kg_grp.at[gm], kg_grp.at[gm], s_kg.at[i], r_kg.at[gm], gpeer((gm + i) % 4))
        cp.start()
        sends.append(cp)

    dq_acc[...] = jnp.zeros_like(dq_acc)
    gfc[0:D, :] = jnp.zeros((D, NQ), BF16)
    m_run[1:2, :] = delta

    def backward(n, carry):
        at = pl.ds(pl.multiple_of(n * CK, CK), CK)
        lanes = pl.ds(pl.multiple_of((n % per_g) * CK, CK), CK)
        g = n // per_g
        f = jnp.exp(m_all[n, 0:1, :] - m_run[0:1, :]) * l_run[0:1, :]
        gf = (dot_t[...].astype(F32) * f).astype(BF16)
        gfc[D : 2 * D, :] = gf
        dp_t = dot(kvn[at, :], gfc[...])
        wb = w_all[at, :]
        ds = (wb.astype(F32) * (dp_t - m_run[1:2, :] * f)).astype(BF16)
        dq_acc[...] = dq_acc[...] + dot(kvt[g, 0:D, lanes], ds)
        part[g, 0:D, lanes] = (dot(qt[...], ds, NT) * (D ** -0.5)).astype(BF16)
        part[g, D : 2 * D, lanes] = dot(gf, wb, NT).astype(BF16)
        return carry

    lax.fori_loop(0, 4 * per_g, backward, 0)

    for i in range(1, 4):
        g = (gm + i) % 4
        cp = rcopy(part.at[g], gred.at[gm], s_p.at[i], r_p.at[gm], gpeer(g))
        cp.start()
        sends.append(cp)

    for j in range(Z):
        dq_s[j] = (dq_acc[:, j * R : (j + 1) * R] * (D ** -0.5)).astype(BF16)
    for i in zorder:
        p = (z + i) % Z
        cp = rcopy(dq_s.at[p], rcv_q.at[z], s_dq.at[i], r_dq.at[z], zpeer(p))
        cp.start()
        sends.append(cp)
    rcv_q[z] = dq_s[z]

    for i in range(1, 4):
        g = (gm + i) % 4
        rcopy(kg_grp.at[g], kg_grp.at[g], s_kg.at[i], r_kg.at[g], gpeer(g)).wait_recv()
    kg_dp[dp] = (kg_grp[0] + kg_grp[1]) + (kg_grp[2] + kg_grp[3])
    for i in range(1, NDP):
        cp = rcopy(kg_dp.at[dp], kg_dp.at[dp], s_kg.at[4 + i], r_kg.at[4 + dp], ((dp + i) % NDP, me))
        cp.start()
        sends.append(cp)

    gred[gm] = part[gm]
    for i in range(1, 4):
        g = (gm + i) % 4
        rcopy(part.at[g], gred.at[g], s_p.at[i], r_p.at[g], gpeer(g)).wait_recv()
    for j in range(Z):
        at = slice(j * R, (j + 1) * R)
        total = (gred[0, :, at].astype(F32) + gred[1, :, at].astype(F32)) + (
            gred[2, :, at].astype(F32) + gred[3, :, at].astype(F32)
        )
        kv_s[j] = total.astype(BF16)
    for i in zorder:
        p = (z + i) % Z
        cp = rcopy(kv_s.at[p], rcv_kv.at[z], s_o.at[i], r_o.at[z], zpeer(p))
        cp.start()
        sends.append(cp)
    rcv_kv[z] = kv_s[z]

    for i in range(1, NDP):
        p = (dp + i) % NDP
        rcopy(kg_dp.at[p], kg_dp.at[p], s_kg.at[4 + i], r_kg.at[4 + p], (p, me)).wait_recv()
    total = kg_dp[0]
    for i in range(1, NDP):
        total = total + kg_dp[i]
    kg_z[z] = total
    for i in zorder:
        p = (z + i) % Z
        cp = rcopy(kg_z.at[z], kg_z.at[z], s_kg.at[4 + NDP + i], r_kg.at[4 + NDP + z], zpeer(p))
        cp.start()
        sends.append(cp)

    def turned_out(a):
        return a.astype(F32).reshape(Z * D, R).T.astype(BF16)

    for i in zorder:
        p = (z + i) % Z
        rcopy(mix_s.at[p], rcv_m.at[p], s_m.at[i], r_m.at[p], zpeer(p)).wait_recv()
    mix_out[...] = turned_out(rcv_m[...])
    for i in zorder:
        p = (z + i) % Z
        rcopy(dq_s.at[p], rcv_q.at[p], s_dq.at[i], r_dq.at[p], zpeer(p)).wait_recv()
    dq_out[...] = turned_out(rcv_q[...])
    for i in zorder:
        p = (z + i) % Z
        rcopy(kv_s.at[p], rcv_kv.at[p], s_o.at[i], r_o.at[p], zpeer(p)).wait_recv()
    dk_out[...] = turned_out(rcv_kv[:, 0:D, :])
    dv_out[...] = turned_out(rcv_kv[:, D : 2 * D, :])
    for i in zorder:
        p = (z + i) % Z
        rcopy(kg_z.at[p], kg_z.at[p], s_kg.at[4 + NDP + i], r_kg.at[4 + NDP + p], zpeer(p)).wait_recv()
    for h in range(0, Z, 2):
        both = jnp.concatenate([kg_z[h][0:T, 0:D], kg_z[h + 1][0:T, 0:D]], axis=1)
        kg_out[:, h * D : (h + 2) * D] = both

    for cp in sends:
        cp.wait_send()


def per_device(Z, NDP, lengths, q, k, v, g, taps):
    W = Z * D
    NQ = R * Z
    NK = 4 * NQ
    T = taps.shape[0]
    CK = min(512, NQ)
    NC = NK // CK
    vm = pltpu.VMEM
    dma = pltpu.SemaphoreType.DMA
    scratch = [
        vm((Z, 2 * D, R), BF16), vm((Z, D, R), BF16), vm((Z, D, R), BF16),
        vm((4, 2 * D, NQ), BF16), vm((NK, 2 * D), BF16), vm((NK, 2 * D), BF16),
        vm((D, NQ), BF16), vm((2 * D, NQ), BF16),
        vm((Z + 1, 2, D, R), BF16), vm((Z + 1, 2, D, R), BF16),
        vm((D, NQ), BF16), vm((2 * D, NQ), BF16),
        vm((T, D, R), F32), vm((T, D, R), F32), vm((R, W), F32),
        vm((4, 32, R), F32), vm((NDP, 32, R), F32), vm((Z, 32, R), F32), vm((W, R), F32), vm((8, R), F32),
        vm((NK, NQ), BF16), vm((NC, 8, NQ), F32), vm((8, NQ), F32), vm((8, NQ), F32),
        vm((D, NQ), F32), vm((D, NQ), F32),
        vm((Z, D, R), BF16), vm((Z, D, R), BF16),
        vm((4, 2 * D, NQ), BF16), vm((4, 2 * D, NQ), BF16), vm((Z, 2 * D, R), BF16),
        vm((Z, D, R), BF16), vm((Z, D, R), BF16), vm((Z, 2 * D, R), BF16),
        dma((Z,)), dma((Z,)), dma((Z,)), dma((Z,)), dma((Z,)), dma((Z,)),
        dma((4,)), dma((4,)), dma((4,)), dma((4,)),
        dma((4 + NDP + Z,)), dma((4 + NDP + Z,)), dma((Z,)), dma((Z,)), dma((Z,)), dma((Z,)),
        dma((4,)), dma((4,)), dma((Z,)), dma((Z,)),
    ]
    vspec = pl.BlockSpec(memory_space=pltpu.VMEM)
    outs = pl.pallas_call(
        functools.partial(kernel, Z, NDP, CK),
        out_shape=(
            jax.ShapeDtypeStruct((R, W), BF16), jax.ShapeDtypeStruct((R, W), BF16),
            jax.ShapeDtypeStruct((R, W), BF16), jax.ShapeDtypeStruct((R, W), BF16),
            jax.ShapeDtypeStruct((T, W), F32),
        ),
        in_specs=[pl.BlockSpec(memory_space=pltpu.SMEM)] + [vspec] * 5,
        out_specs=(vspec,) * 5,
        scratch_shapes=scratch,
        compiler_params=pltpu.CompilerParams(
            collective_id=0, has_side_effects=True, vmem_limit_bytes=56 * 1024 * 1024
        ),
        cost_estimate=pl.CostEstimate(
            flops=12 * NQ * NK * D, bytes_accessed=9 * R * W * 2, transcendentals=NQ * NK
        ),
    )(lengths, q[0], k[0], v[0], g[0], taps)
    return outs[0][None], outs[1][None], outs[2][None], outs[3][None], outs[4]


def solution(mesh):
    Z = mesh.shape["ctx"] // 4
    NDP = mesh.shape["dp"]
    split = P("dp", "ctx", None)
    return jax.shard_map(
        functools.partial(per_device, Z, NDP),
        mesh=mesh,
        in_specs=(P(), split, split, split, split, P()),
        out_specs=(split, split, split, split, P()),
        check_vma=False,
    )
```

time: 436 us -> 91.1 us (0.21)
  waiting for transfers between devices: 147 us -> 0 us
  blocking collectives: 143 us -> 0 us
  Pallas kernels: 0 us -> 85.2 us
  matrix products: 64.5 us -> 0 us
  local copies, waits for them, and re-layouts: 32.8 us -> 5 us
  other arithmetic: 22.4 us -> 0 us
  between operations: 14 us -> 0.65 us
  starting transfers between devices: 12.1 us -> 0 us
    all_gather x4 -> x0, waiting for transfers between devices: 142 us -> none  [the longest x1 65.6 us: per_device(): lax.all_gather(value_states, 'ctx', axis=1, tiled=True)]
    pallas_call x0 -> x1, Pallas kernels: none -> 85.2 us  [per_device(): pl.pallas_call(functools.partial(kernel, Z, NDP, CK), out_shape=(jax.Shap...]
    psum x1 -> x0, blocking collectives: 75.4 us -> none  [per_device(): kernel_grad = lax.psum(jnp.stack(kernel_terms), ('dp', 'ctx'))]
    all_gather x2 -> x0, blocking collectives: 67.4 us -> none  [the longest x1 34.3 us: per_device(): lax.all_gather(delta_rows, 'ctx', axis=1, tiled=True)]
    dot_general x7 -> x0, matrix products: 64.5 us -> none  [the longest x1 14.1 us: tile_terms(): jnp.einsum('qhd,khd->hqk', grad_rows, value_rows, preferred_element_type=...]
    all_gather x3 -> x0, local copies, waits for them, and re-layouts: 19.2 us -> none  [the longest x1 6.44 us: per_device(): lax.all_gather(value_states, 'ctx', axis=1, tiled=True)]
    reduce_sum x6 -> x0, other arithmetic: 16 us -> none  [the longest x1 5.23 us: per_device(): jnp.sum((out_grad.astype(jnp.float32) * attention.astype(jnp.float32)).re...]
    ppermute x4 -> x0, starting transfers between devices: 12 us -> none  [the longest x2 7.94 us: extended(): lax.ppermute(lax.slice_in_dim(block, block.shape[dim] - width, None, axis...]
  transfers between devices with their start and end apart: 8 -> 0, of which waited for: 5 -> 0; matrix products, arithmetic and copies ran while one was open for 20% -> 0% of each run, Pallas kernels for 0% -> 0%
where the time goes in v1:
time: 91.1 us; the launch traced here: 90.9 us
  Pallas kernels  85.2 us (94%)
  local copies, waits for them, and re-layouts  5 us (5%)
    pallas_call x1, Pallas kernels, per_device(): pl.pallas_call(functools.partial(kernel, Z, NDP, CK), out_shape=(jax.Shap...  85.2 us
    unnamed x13, local copies, waits for them, and re-layouts  5 us

profile of v1, /device:TPU:1, one launch (start us, length us, event | category | flops | bytes accessed | tf_op | source)
XLA Modules:
  0.0 90.9 jit_solution(5479312487016180016)
XLA Ops:
  0.6 85.2 %shard_map.101 = (bf16[128,512]{1,0:T(8,128)(2,1)}, bf16[128,512]{1,0:T(8,128)(2,1)}, bf16[128,512]{1,0:T(8,128)(2,1)}, bf16[128,512]{1,0:T(8,128)(2,1)}, f32[31,512]{1,0:T(8,128)}) custom-call(s32[8]{0:T(128)} %len_ref.1, bf16[128,512]{1,0:T(8,128)(2,1)} %bitcast.12, bf16[128,512]{1,0:T(8,128)(2,1)} %bitcast.13, bf16[128,512]{1,0:T(8,128)(2,1)} %bitcast.14, ...), custom_call_target="tpu_custom_call" | custom-call | flops 3221225472 | bytes 1179648 | tf_op jit(solution)/shard_map/pallas_call | solution.py:409
  85.8 0.0 copy-start.2
  85.9 1.6 %copy.16 = bf16[1,128,512]{2,1,0:T(8,128)(2,1)} copy(bf16[1,128,512]{2,1,0:T(8,128)(2,1)} %bitcast.11) | data formatting | bytes 262144
  87.5 0.0 copy-done.2
  87.5 0.0 copy-start.1
  87.5 0.7 copy.17
  88.1 0.3 copy-done.1
  88.4 0.0 copy-start
  88.4 0.7 copy.18
  89.1 0.3 copy-done
  89.4 0.0 copy-start.3
  89.4 0.7 copy.19
  90.0 0.2 copy-done.3
  90.2 0.6 copy.20
Async XLA Ops:
  85.8 1.6 %copy-start.2 = (bf16[128,512]{1,0:T(8,128)(2,1)S(1)}, bf16[128,512]{1,0:T(8,128)(2,1)}, u32[]{:S(2)}) copy-start(bf16[128,512]{1,0:T(8,128)(2,1)} %get-tuple-element.11) | copy-start | bytes 393220
  87.5 1.0 %copy-start.1 = (bf16[128,512]{1,0:T(8,128)(2,1)S(1)}, bf16[128,512]{1,0:T(8,128)(2,1)}, u32[]{:S(2)}) copy-start(bf16[128,512]{1,0:T(8,128)(2,1)} %get-tuple-element.12) | copy-start | bytes 393220
  88.4 1.0 %copy-start = (bf16[128,512]{1,0:T(8,128)(2,1)S(1)}, bf16[128,512]{1,0:T(8,128)(2,1)}, u32[]{:S(2)}) copy-start(bf16[128,512]{1,0:T(8,128)(2,1)} %get-tuple-element.13) | copy-start | bytes 393220
  89.4 0.9 copy-start.3

commit v2 on v1

v2 whole, which is shorter than its diff:
```python
import functools

import jax
import jax.numpy as jnp
from jax import lax
from jax.experimental import pallas as pl
from jax.experimental.pallas import tpu as pltpu
from jax.sharding import PartitionSpec as P

MESH = pl.DeviceIdType.MESH
D = 64
R = 128
FILL = -1e30
F32 = jnp.float32
BF16 = jnp.bfloat16

NN = (((1,), (0,)), ((), ()))
NT = (((1,), (1,)), ((), ()))


def dot(a, b, dims=NN):
    return lax.dot_general(a, b, dims, preferred_element_type=F32)


def kernel(
    Z, NDP,
    len_ref, q_hbm, k_hbm, v_hbm, g_hbm, ck_hbm,
    land, kg_land,
    q_in, k_in, v_in, g_in, ck_in,
    snd_kv, snd_q, snd_g, kvt, kvn, kaug, qt, qaug, gseq, oseq, dot_t, gfc,
    kb, kga, kgt, kg_grp, kg_dp, kg_s, kg_s1,
    w_all, m_all, m_run, l_run, acc, dq_acc, mix_s, dq_s, part, gred, kv_s,
    s_in, s_kv, r_kv, s_q, r_q, s_g, r_g, s_grp, r_grp, s_h, r_h,
    s_kg, r_kg, s_m, r_m, s_dq, r_dq, s_p, r_p, s_o, r_o, s_loc,
):
    NQ = R * Z
    CK = 4 * R
    T = ck_in.shape[0]
    HALF = (T - 1) // 2
    me = lax.axis_index("ctx")
    dp = lax.axis_index("dp")
    x = me // (2 * Z)
    z = (me // 2) % Z
    c = me % 2
    gm = 2 * x + c
    length = len_ref[dp]

    def zpeer(p):
        return (dp, x * 2 * Z + 2 * p + c)

    def gpeer(g):
        return (dp, (g // 2) * 2 * Z + 2 * z + g % 2)

    def rcopy(src, dst, ssem, rsem, dev):
        return pltpu.make_async_remote_copy(
            src_ref=src, dst_ref=dst, send_sem=ssem, recv_sem=rsem, device_id=dev, device_id_type=MESH
        )

    offs = [0]
    for i in range(1, Z // 2 + 1):
        offs.append(i)
        if Z - i != i:
            offs.append(Z - i)
    zorder = offs[1:]
    slot_of = {o: n for n, o in enumerate(offs)}

    def off_of(n):
        odd = n % 2
        return odd * ((n + 1) // 2) + (1 - odd) * ((Z - n // 2) % Z)

    zero_blk = jnp.zeros((D, R), BF16)
    for s in (gseq, oseq):
        s[0, 0] = zero_blk
        s[Z, 1] = zero_blk

    barrier = pltpu.get_barrier_semaphore()
    for i in range(1, Z):
        pl.semaphore_signal(barrier, inc=1, device_id=zpeer((z + i) % Z), device_id_type=MESH)
    for i in range(1, 4):
        pl.semaphore_signal(barrier, inc=1, device_id=gpeer((gm + i) % 4), device_id_type=MESH)
    for i in range(1, NDP):
        pl.semaphore_signal(barrier, inc=1, device_id=((dp + i) % NDP, me), device_id_type=MESH)

    loads = []
    for n, (a, b) in enumerate(((g_hbm, g_in), (q_hbm, q_in), (k_hbm, k_in), (v_hbm, v_in), (ck_hbm, ck_in))):
        cp = pltpu.make_async_copy(a, b, s_in.at[n])
        cp.start()
        loads.append(cp)

    my_frames = me * R + lax.broadcasted_iota(jnp.int32, (1, R), 1)
    my_live = (my_frames < length).astype(F32)
    turned = lambda ref: ref[...].astype(F32).T
    loads[0].wait()
    snd_g[...] = (turned(g_in) * my_live).astype(BF16).reshape(Z, D, R)
    loads[1].wait()
    snd_q[...] = turned(q_in).astype(BF16).reshape(Z, D, R)
    loads[2].wait()
    snd_kv[:, 0, :, :] = turned(k_in).astype(BF16).reshape(Z, D, R)
    loads[3].wait()
    snd_kv[:, 1, :, :] = turned(v_in).astype(BF16).reshape(Z, D, R)
    loads[4].wait()

    kgt[...] = jnp.zeros_like(kgt)
    kgt[0:T, :] = ck_in[...]
    for b in range(Z * D // R):
        kg_s1[b * R : (b + 1) * R, :] = kgt[:, b * R : (b + 1) * R].T
    my_taps = kg_s1[pl.ds(pl.multiple_of(z * D, D), D), :]
    for t in range(T):
        kb[t] = jnp.broadcast_to(my_taps[:, t : t + 1], (D, R))
    kga[...] = jnp.zeros_like(kga)
    m_run[...] = jnp.full(m_run.shape, FILL, F32)
    l_run[...] = jnp.zeros_like(l_run)
    acc[...] = jnp.zeros_like(acc)
    dq_acc[...] = jnp.zeros_like(dq_acc)
    gfc[0:D, :] = jnp.zeros((D, NQ), BF16)
    row = lax.broadcasted_iota(jnp.int32, (D, NQ), 0)
    qaug[D : 2 * D, :] = jnp.where(row == 0, 1.0, 0.0).astype(BF16)

    pl.semaphore_wait(barrier, (Z - 1) + 3 + (NDP - 1))

    def cols(j):
        return pl.ds(pl.multiple_of(j * R, R), R)

    def seq_at(ref, p):
        return ref.at[p // 2, p % 2]

    def kv_at(n, g):
        return kvt.at[n, :, :, cols(g)]

    sends = []

    def send(cp):
        cp.start()
        sends.append(cp)

    for i in zorder:
        p = (z + i) % Z
        send(rcopy(snd_g.at[p], seq_at(gseq, 1 + 2 * z + c), s_g.at[i], r_g.at[z], zpeer(p)))
    for i in zorder:
        p = (z + i) % Z
        send(rcopy(snd_q.at[p], qt.at[:, cols(z)], s_q.at[i], r_q.at[z], zpeer(p)))
    for i in zorder:
        p = (z + i) % Z
        n = slot_of[Z - i]
        send(rcopy(snd_kv.at[p], kv_at(n, gm), s_kv.at[i], r_kv.at[n], zpeer(p)))
    kvt[0, :, :, cols(gm)] = snd_kv[z]
    qt[:, cols(z)] = snd_q[z]
    gseq[(1 + 2 * z + c) // 2, (1 + 2 * z + c) % 2] = snd_g[z]

    def share(n):
        for i in range(1, 4):
            rcopy(kv_at(n, gm), kv_at(n, gm), s_grp.at[n, i], r_grp.at[n, gm], gpeer((gm + i) % 4)).start()

    share(0)

    for i in zorder:
        p = (z + i) % Z
        rcopy(snd_g.at[p], seq_at(gseq, 1 + 2 * p + c), s_g.at[i], r_g.at[p], zpeer(p)).wait_recv()

    def halo(seq, n):
        mine = seq.at[pl.ds(c, Z), 1 - c]
        rcopy(mine, mine, s_h.at[n], r_h.at[n], gpeer(gm + 1 - 2 * c)).start()

        @pl.when(x != c)
        def _():
            rcopy(
                seq.at[c * Z, 1 - c], seq.at[(1 - c) * Z, 1 - c],
                s_h.at[n + 1], r_h.at[n + 1], gpeer(3 - gm),
            ).start()

    def halo_wait(seq, n):
        mine = seq.at[pl.ds(c, Z), 1 - c]
        other = seq.at[pl.ds(1 - c, Z), c]
        cp = rcopy(mine, other, s_h.at[n], r_h.at[n], gpeer(gm + 1 - 2 * c))
        cp.wait_send()
        cp.wait_recv()

        @pl.when(x != c)
        def _():
            cp2 = rcopy(
                seq.at[c * Z, 1 - c], seq.at[c * Z, c],
                s_h.at[n + 1], r_h.at[n + 1], gpeer(3 - gm),
            )
            cp2.wait_send()
            cp2.wait_recv()

    halo(gseq, 0)

    lane = lax.broadcasted_iota(jnp.int32, (1, R), 1)

    def live_of(j):
        return ((x * 2 * Z + 2 * j + c) * R + lane < length).astype(F32)

    def window(seq, j):
        p = 1 + 2 * j + c
        parts = [seq[(p + d) // 2, (p + d) % 2].astype(F32) for d in (-1, 0, 1)]
        return jnp.concatenate(parts, axis=1), parts[1]

    def shifted(wide, s):
        if s == 0:
            return wide[:, R : 2 * R]
        return pltpu.roll(wide, (3 * R - s) % (3 * R), 1)[:, R : 2 * R]

    def grad_block(j, carry):
        wide, mid = window(gseq, j)
        total = mid
        for t in range(T):
            total = total + kb[t] * shifted(wide, HALF - t)
        dot_t[:, cols(j)] = (total * live_of(j)).astype(BF16)
        return carry

    halo_wait(gseq, 0)
    lax.fori_loop(0, Z, grad_block, 0)

    for i in zorder:
        p = (z + i) % Z
        rcopy(snd_q.at[p], qt.at[:, cols(p)], s_q.at[i], r_q.at[p], zpeer(p)).wait_recv()
    qaug[0:D, :] = (qt[...].astype(F32) * (D ** -0.5)).astype(BF16)

    lane_full = lax.broadcasted_iota(jnp.int32, (R, R), 1)
    sub_full = lax.broadcasted_iota(jnp.int32, (R, R), 0)

    def keys_at(n):
        return pl.ds(pl.multiple_of(n * CK, CK), CK)

    def forward(n, carry):
        @pl.when(n < Z)
        def _():
            rcopy(kv_at(n, gm), kv_at(n, gm), s_kv.at[0], r_kv.at[n], gpeer(gm)).wait_recv()
            share(n)

        m = n - 1
        zs = (z + off_of(m)) % Z
        for i in range(1, 4):
            g = (gm + i) % 4
            rcopy(kv_at(m, g), kv_at(m, g), s_grp.at[m, i], r_grp.at[m, g], gpeer(g)).wait_recv()
        for g in range(4):
            blk = kvt[m, :, :, g * R : (g + 1) * R].reshape(2 * D, R).astype(F32).T
            at = pl.ds(pl.multiple_of(m * CK + g * R, R), R)
            kvn[at, :] = blk.astype(BF16)
            frame = ((g // 2) * 2 * Z + 2 * zs + g % 2) * R + sub_full
            fill = jnp.where((lane_full == D) & (frame >= length), FILL, 0.0)
            kaug[at, :] = jnp.where(lane_full < D, blk, fill).astype(BF16)
        at = keys_at(m)
        s = dot(kaug[at, :], qaug[...])
        m_old = m_run[0:1, :]
        m_new = jnp.maximum(m_old, jnp.max(s, axis=0, keepdims=True))
        w = jnp.exp(s - m_new)
        alpha = jnp.exp(m_old - m_new)
        l_run[0:1, :] = l_run[0:1, :] * alpha + jnp.sum(w, axis=0, keepdims=True)
        wb = w.astype(BF16)
        w_all[at, :] = wb
        acc[...] = acc[...] * alpha + dot(kvt[m, 1], wb)
        m_run[0:1, :] = m_new
        m_all[m, 0:1, :] = m_new
        return carry

    lax.fori_loop(1, Z + 1, forward, 0)

    inv = 1.0 / l_run[0:1, :]
    l_run[0:1, :] = inv
    att = (acc[...] * inv).astype(BF16)
    for j in range(Z):
        blk = (att[:, j * R : (j + 1) * R].astype(F32) * live_of(j)).astype(BF16)
        oseq[(1 + 2 * j + c) // 2, (1 + 2 * j + c) % 2] = blk
    halo(oseq, 2)
    m_run[1:2, :] = jnp.sum(dot_t[...].astype(F32) * att.astype(F32), axis=0, keepdims=True)

    def out_block(j, carry):
        wide, mid = window(oseq, j)
        p = 1 + 2 * j + c
        grad = gseq[p // 2, p % 2].astype(F32)
        total = mid
        for t in range(T):
            seg = shifted(wide, t - HALF)
            total = total + kb[t] * seg
            kga[t] = kga[t] + grad * seg
        mix_s[j] = (total * live_of(j)).astype(BF16)
        return carry

    def mix_copy(i, p, h):
        return rcopy(mix_s.at[p], land.at[h, 0], s_m.at[i], r_m.at[h], zpeer(p))

    def taps_a(i):
        g = (gm + i) % 4
        return rcopy(kg_grp.at[gm], kg_grp.at[gm], s_kg.at[i], r_kg.at[gm], gpeer(g))

    def taps_a_in(i):
        g = (gm + i) % 4
        return rcopy(kg_grp.at[g], kg_grp.at[g], s_kg.at[i], r_kg.at[g], gpeer(g))

    def taps_b(i):
        return rcopy(kg_dp.at[dp], kg_dp.at[dp], s_kg.at[4 + i], r_kg.at[4 + dp], ((dp + i) % NDP, me))

    def taps_b_in(i):
        p = (dp + i) % NDP
        return rcopy(kg_dp.at[p], kg_dp.at[p], s_kg.at[4 + i], r_kg.at[4 + p], (p, me))

    def taps_c(i, p, h):
        return rcopy(kg_s, kg_land.at[h], s_kg.at[4 + NDP + i], r_kg.at[4 + NDP + h], zpeer(p))

    def part_copy(n, i):
        g = (gm + i) % 4
        return rcopy(part.at[n, :, :, cols(g)], gred.at[n, gm], s_p.at[n, i], r_p.at[n, gm], gpeer(g))

    def part_in(n, i):
        g = (gm + i) % 4
        return rcopy(part.at[n, :, :, cols(g)], gred.at[n, g], s_p.at[n, i], r_p.at[n, g], gpeer(g))

    def add_up(n):
        for i in range(1, 4):
            part_in(n, i).wait_recv()
        gred[n, gm] = part[n, :, :, cols(gm)]
        total = (gred[n, 0].astype(F32) + gred[n, 1].astype(F32)) + (
            gred[n, 2].astype(F32) + gred[n, 3].astype(F32)
        )
        kv_s[n] = total.astype(BF16)

    def kv_copy(n, h):
        return rcopy(kv_s.at[n], land.at[h, pl.ds(2, 2)], s_o.at[n], r_o.at[h], zpeer((z + off_of(n)) % Z))

    def backward(k, carry):
        n = Z - 1 - k
        at = keys_at(n)
        f = jnp.exp(m_all[n, 0:1, :] - m_run[0:1, :]) * l_run[0:1, :]
        gf = (dot_t[...].astype(F32) * f).astype(BF16)
        gfc[D : 2 * D, :] = gf
        dp_t = dot(kvn[at, :], gfc[...])
        wb = w_all[at, :]
        ds = (wb.astype(F32) * (dp_t - m_run[1:2, :] * f)).astype(BF16)
        part[n, 0] = (dot(qt[...], ds, NT) * (D ** -0.5)).astype(BF16)
        part[n, 1] = dot(gf, wb, NT).astype(BF16)
        for i in range(1, 4):
            part_copy(n, i).start()
        dq_acc[...] = dq_acc[...] + dot(kvt[n, 0], ds)

        @pl.when(k > 0)
        def _():
            add_up(n + 1)
            kv_copy(n + 1, z).start()

        @pl.when(k == 0)
        def _():
            halo_wait(oseq, 2)
            lax.fori_loop(0, Z, out_block, 0)
            for i in zorder:
                mix_copy(i, (z + i) % Z, z).start()
            lane_d = lax.broadcasted_iota(jnp.int32, (D, R), 1)
            red = jnp.zeros((D, R), F32)
            for t in range(T):
                red = jnp.where(lane_d == t, jnp.sum(kga[t], axis=1, keepdims=True), red)
            kg_grp[gm] = jnp.concatenate([red, jnp.zeros((R - D, R), F32)], axis=0).T[0:32, :]
            for i in range(1, 4):
                taps_a(i).start()

        @pl.when(k == (Z + 1) // 3)
        def _():
            for i in range(1, 4):
                taps_a_in(i).wait_recv()
            kg_dp[dp] = (kg_grp[0] + kg_grp[1]) + (kg_grp[2] + kg_grp[3])
            for i in range(1, NDP):
                taps_b(i).start()

        @pl.when(k == Z - 2)
        def _():
            for i in range(1, NDP):
                taps_b_in(i).wait_recv()
            total = kg_dp[0]
            for i in range(1, NDP):
                total = total + kg_dp[i]
            kg_s[...] = total
            for i in zorder:
                taps_c(i, (z + i) % Z, z).start()

        return carry

    lax.fori_loop(0, Z, backward, 0)

    for j in range(Z):
        dq_s[j] = (dq_acc[:, j * R : (j + 1) * R] * (D ** -0.5)).astype(BF16)

    def dq_copy(i, p, h):
        return rcopy(dq_s.at[p], land.at[h, 1], s_dq.at[i], r_dq.at[h], zpeer(p))

    for i in zorder:
        dq_copy(i, (z + i) % Z, z).start()
    add_up(0)
    local = [
        pltpu.make_async_copy(mix_s.at[z], land.at[z, 0], s_loc.at[0]),
        pltpu.make_async_copy(dq_s.at[z], land.at[z, 1], s_loc.at[1]),
        pltpu.make_async_copy(kv_s.at[0], land.at[z, pl.ds(2, 2)], s_loc.at[2]),
        pltpu.make_async_copy(kg_s, kg_land.at[z], s_loc.at[3]),
    ]
    for cp in local:
        cp.start()

    for cp in sends:
        cp.wait_send()

    def drain(n, carry):
        for i in range(1, 4):
            rcopy(kv_at(n, gm), kv_at(n, gm), s_grp.at[n, i], r_grp.at[n, gm], gpeer((gm + i) % 4)).wait_send()
            part_copy(n, i).wait_send()
        return carry

    lax.fori_loop(0, Z, drain, 0)
    for i in range(1, 4):
        taps_a(i).wait_send()
    for i in range(1, NDP):
        taps_b(i).wait_send()
    for i in zorder:
        p = (z + i) % Z
        for cp in (mix_copy(i, p, p), taps_c(i, p, p), dq_copy(i, p, p)):
            cp.wait_send()
            cp.wait_recv()
        kv_copy(slot_of[i], p).wait_send()
        kv_copy(slot_of[i], p).wait_recv()
    for cp in local:
        cp.wait()


def finish(Z, T, land, kg, mix_out, dq_out, dk_out, dv_out, kg_out):
    for n, out in enumerate((mix_out, dq_out, dk_out, dv_out)):
        out[...] = land[:, n].astype(F32).reshape(Z * D, R).T.astype(BF16)
    for h in range(0, Z, 2):
        both = jnp.concatenate([kg[h][0:T, 0:D], kg[h + 1][0:T, 0:D]], axis=1)
        kg_out[:, h * D : (h + 2) * D] = both


def per_device(Z, NDP, lengths, q, k, v, g, taps):
    W = Z * D
    NQ = R * Z
    NK = 4 * NQ
    T = taps.shape[0]
    CK = 4 * R
    vm = pltpu.VMEM
    dma = pltpu.SemaphoreType.DMA
    scratch = [
        vm((R, W), BF16), vm((R, W), BF16), vm((R, W), BF16), vm((R, W), BF16), vm((T, W), F32),
        vm((Z, 2, D, R), BF16), vm((Z, D, R), BF16), vm((Z, D, R), BF16),
        vm((Z, 2, D, CK), BF16), vm((NK, 2 * D), BF16), vm((NK, 2 * D), BF16),
        vm((D, NQ), BF16), vm((2 * D, NQ), BF16),
        vm((Z + 1, 2, D, R), BF16), vm((Z + 1, 2, D, R), BF16),
        vm((D, NQ), BF16), vm((2 * D, NQ), BF16),
        vm((T, D, R), F32), vm((T, D, R), F32), vm((R, W), F32),
        vm((4, 32, R), F32), vm((NDP, 32, R), F32), vm((32, R), F32), vm((W, R), F32),
        vm((NK, NQ), BF16), vm((Z, 8, NQ), F32), vm((8, NQ), F32), vm((8, NQ), F32),
        vm((D, NQ), F32), vm((D, NQ), F32),
        vm((Z, D, R), BF16), vm((Z, D, R), BF16),
        vm((Z, 2, D, CK), BF16), vm((Z, 4, 2, D, R), BF16), vm((Z, 2, D, R), BF16),
        dma((5,)),
        dma((Z,)), dma((Z,)), dma((Z,)), dma((Z,)), dma((Z,)), dma((Z,)),
        dma((Z, 4)), dma((Z, 4)), dma((4,)), dma((4,)),
        dma((4 + NDP + Z,)), dma((4 + NDP + Z,)), dma((Z,)), dma((Z,)), dma((Z,)), dma((Z,)),
        dma((Z, 4)), dma((Z, 4)), dma((Z,)), dma((Z,)), dma((4,)),
    ]
    vspec = pl.BlockSpec(memory_space=pltpu.VMEM)
    anyspec = pl.BlockSpec(memory_space=pl.ANY)
    land, kg = pl.pallas_call(
        functools.partial(kernel, Z, NDP),
        out_shape=(
            jax.ShapeDtypeStruct((Z, 4, D, R), BF16),
            jax.ShapeDtypeStruct((Z, 32, R), F32),
        ),
        in_specs=[pl.BlockSpec(memory_space=pltpu.SMEM)] + [anyspec] * 5,
        out_specs=(anyspec, anyspec),
        scratch_shapes=scratch,
        compiler_params=pltpu.CompilerParams(
            collective_id=0, has_side_effects=True, vmem_limit_bytes=56 * 1024 * 1024
        ),
        cost_estimate=pl.CostEstimate(
            flops=12 * NQ * NK * D, bytes_accessed=9 * R * W * 2, transcendentals=NQ * NK
        ),
    )(lengths, q[0], k[0], v[0], g[0], taps)
    outs = pl.pallas_call(
        functools.partial(finish, Z, T),
        out_shape=(
            jax.ShapeDtypeStruct((R, W), BF16), jax.ShapeDtypeStruct((R, W), BF16),
            jax.ShapeDtypeStruct((R, W), BF16), jax.ShapeDtypeStruct((R, W), BF16),
            jax.ShapeDtypeStruct((T, W), F32),
        ),
        in_specs=[vspec] * 2,
        out_specs=(vspec,) * 5,
    )(land, kg)
    return outs[0][None], outs[1][None], outs[2][None], outs[3][None], outs[4]


def solution(mesh):
    Z = mesh.shape["ctx"] // 4
    NDP = mesh.shape["dp"]
    split = P("dp", "ctx", None)
    return jax.shard_map(
        functools.partial(per_device, Z, NDP),
        mesh=mesh,
        in_specs=(P(), split, split, split, split, P()),
        out_specs=(split, split, split, split, P()),
        check_vma=False,
    )
```

time: 91.1 us -> 74.1 us (0.81)
  Pallas kernels: 85.2 us -> 73.3 us
  local copies, waits for them, and re-layouts: 5 us -> 0 us
    pallas_call x1 -> x2, Pallas kernels: 85.2 us -> 73.3 us  [the longest x1 71.4 us: per_device(): pl.pallas_call(functools.partial(kernel, Z, NDP), out_shape=(jax.ShapeDty...]
    unnamed x13 -> x0, local copies, waits for them, and re-layouts: 5 us -> none
where the time goes in v2:
time: 74.1 us; the launch traced here: 74 us
  Pallas kernels  73.3 us (99%)
    pallas_call x1, Pallas kernels, per_device(): pl.pallas_call(functools.partial(kernel, Z, NDP), out_shape=(jax.ShapeDty...  71.4 us
    pallas_call x1, Pallas kernels, per_device(): pl.pallas_call(functools.partial(finish, Z, T), out_shape=(jax.ShapeDtype...  1.97 us

profile of v2, /device:TPU:1, one launch (start us, length us, event | category | flops | bytes accessed | tf_op | source)
XLA Modules:
  0.0 74.0 jit_solution(11372438757991765838)
XLA Ops:
  0.6 71.4 %shard_map.101 = (bf16[8,4,64,128]{3,2,1,0:T(8,128)(2,1)}, f32[8,32,128]{2,1,0:T(8,128)}) custom-call(s32[8]{0:T(128)} %len_ref.1, bf16[128,512]{1,0:T(8,128)(2,1)} %bitcast.8, bf16[128,512]{1,0:T(8,128)(2,1)} %bitcast.9, bf16[128,512]{1,0:T(8,128)(2,1)} %bitcast.10, bf16[128,512]{1,0:T(8,128)(2,1)} %bitcast.11, f32[31,512]{1,0:T(8,128)} %ck_hbm.1), custom_call_target="tpu_custom_call" | custom-call | flops 3221225472 | bytes 1179648 | tf_op jit(solution)/shard_map/pallas_call | solution.py:459
  72.0 2.0 %shard_map.102 = (bf16[128,512]{1,0:T(8,128)(2,1)}, bf16[128,512]{1,0:T(8,128)(2,1)}, bf16[128,512]{1,0:T(8,128)(2,1)}, bf16[128,512]{1,0:T(8,128)(2,1)}, f32[31,512]{1,0:T(8,128)}) custom-call(bf16[8,4,64,128]{3,2,1,0:T(8,128)(2,1)} %get-tuple-element.12.land, f32[8,32,128]{2,1,0:T(8,128)} %get-tuple-element.13.kg), custom_call_target="tpu_custom_call" | custom-call | tf_op jit(solution)/shard_map/pallas_call | solution.py:475

commit v3 on v2

--- a/solution.py
+++ b/solution.py
@@ -27,10 +27,10 @@
     len_ref, q_hbm, k_hbm, v_hbm, g_hbm, ck_hbm,
     land, kg_land,
     q_in, k_in, v_in, g_in, ck_in,
-    snd_kv, snd_q, snd_g, kvt, kvn, kaug, qt, qaug, gseq, oseq, dot_t, gfc,
+    snd_kv, snd_q, snd_g, snd_d, gx, gh, gbuf, kvt, kvn, kaug, qt, qaug, oseq, dot_t, gfc,
     kb, kga, kgt, kg_grp, kg_dp, kg_s, kg_s1,
     w_all, m_all, m_run, l_run, acc, dq_acc, mix_s, dq_s, part, gred, kv_s,
-    s_in, s_kv, r_kv, s_q, r_q, s_g, r_g, s_grp, r_grp, s_h, r_h,
+    s_in, s_kv, r_kv, s_q, r_q, s_g, r_g, s_d, r_d, s_grp, r_grp, s_h, r_h,
     s_kg, r_kg, s_m, r_m, s_dq, r_dq, s_p, r_p, s_o, r_o, s_loc,
 ):
     NQ = R * Z
@@ -43,6 +43,10 @@
     z = (me // 2) % Z
     c = me % 2
     gm = 2 * x + c
+    N = 4 * Z
+    sib = gm + 1 - 2 * c
+    across = (gm + 2) % 4
+    across_sib = 3 - gm
     length = len_ref[dp]
 
     def zpeer(p):
@@ -69,9 +73,8 @@
         return odd * ((n + 1) // 2) + (1 - odd) * ((Z - n // 2) % Z)
 
     zero_blk = jnp.zeros((D, R), BF16)
-    for s in (gseq, oseq):
-        s[0, 0] = zero_blk
-        s[Z, 1] = zero_blk
+    oseq[0, 0] = zero_blk
+    oseq[Z, 1] = zero_blk
 
     barrier = pltpu.get_barrier_semaphore()
     for i in range(1, Z):
@@ -80,25 +83,66 @@
         pl.semaphore_signal(barrier, inc=1, device_id=gpeer((gm + i) % 4), device_id_type=MESH)
     for i in range(1, NDP):
         pl.semaphore_signal(barrier, inc=1, device_id=((dp + i) % NDP, me), device_id_type=MESH)
+    pl.semaphore_signal(barrier, inc=1, device_id=(dp, (me + 2 * c - 1 + N) % N), device_id_type=MESH)
 
     loads = []
-    for n, (a, b) in enumerate(((g_hbm, g_in), (q_hbm, q_in), (k_hbm, k_in), (v_hbm, v_in), (ck_hbm, ck_in))):
+    for n, (a, b) in enumerate(((q_hbm, q_in), (k_hbm, k_in), (v_hbm, v_in), (g_hbm, g_in), (ck_hbm, ck_in))):
         cp = pltpu.make_async_copy(a, b, s_in.at[n])
         cp.start()
         loads.append(cp)
 
-    my_frames = me * R + lax.broadcasted_iota(jnp.int32, (1, R), 1)
-    my_live = (my_frames < length).astype(F32)
-    turned = lambda ref: ref[...].astype(F32).T
+    turned = lambda a: a.astype(F32).T.astype(BF16).reshape(Z, D, R)
     loads[0].wait()
-    snd_g[...] = (turned(g_in) * my_live).astype(BF16).reshape(Z, D, R)
+    snd_q[...] = turned(q_in[...])
     loads[1].wait()
-    snd_q[...] = turned(q_in).astype(BF16).reshape(Z, D, R)
+    snd_kv[:, 0, :, :] = turned(k_in[...])
     loads[2].wait()
-    snd_kv[:, 0, :, :] = turned(k_in).astype(BF16).reshape(Z, D, R)
+    snd_kv[:, 1, :, :] = turned(v_in[...])
     loads[3].wait()
-    snd_kv[:, 1, :, :] = turned(v_in).astype(BF16).reshape(Z, D, R)
     loads[4].wait()
+
+    pl.semaphore_wait(barrier, (Z - 1) + 3 + (NDP - 1) + 1)
+
+    def cols(j):
+        return pl.ds(pl.multiple_of(j * R, R), R)
+
+    def seq_at(ref, p):
+        return ref.at[p // 2, p % 2]
+
+    def kv_at(n, g):
+        return kvt.at[n, :, :, cols(g)]
+
+    sends = []
+
+    def send(cp):
+        cp.start()
+        sends.append(cp)
+
+    up, down = (dp, (me + 1) % N), (dp, (me + N - 1) % N)
+    send(rcopy(g_in.at[pl.ds(R - 16, 16)], gh.at[0], s_h.at[0], r_h.at[0], up))
+    send(rcopy(g_in.at[pl.ds(0, 16)], gh.at[1], s_h.at[1], r_h.at[1], down))
+    for i in zorder:
+        p = (z + i) % Z
+        send(rcopy(snd_q.at[p], qt.at[:, cols(z)], s_q.at[i], r_q.at[z], zpeer(p)))
+    for i in zorder:
+        p = (z + i) % Z
+        n = slot_of[Z - i]
+        send(rcopy(snd_kv.at[p], kv_at(n, gm), s_kv.at[i], r_kv.at[n], zpeer(p)))
+    kvt[0, :, :, cols(gm)] = snd_kv[z]
+
+    def grp_copy(n, g, k, to):
+        return rcopy(kv_at(n, g), kv_at(n, g), s_grp.at[n, k], r_grp.at[n, g], gpeer(to))
+
+    def share(n):
+        grp_copy(n, gm, 1, across).start()
+        grp_copy(n, gm, 0, sib).start()
+
+    def relay(n):
+        grp_copy(n, across, 1, across).wait_recv()
+        grp_copy(n, across, 2, sib).start()
+
+    share(0)
+    qt[:, cols(z)] = snd_q[z]
 
     kgt[...] = jnp.zeros_like(kgt)
     kgt[0:T, :] = ck_in[...]
@@ -116,46 +160,38 @@
     row = lax.broadcasted_iota(jnp.int32, (D, NQ), 0)
     qaug[D : 2 * D, :] = jnp.where(row == 0, 1.0, 0.0).astype(BF16)
 
-    pl.semaphore_wait(barrier, (Z - 1) + 3 + (NDP - 1))
-
-    def cols(j):
-        return pl.ds(pl.multiple_of(j * R, R), R)
-
-    def seq_at(ref, p):
-        return ref.at[p // 2, p % 2]
-
-    def kv_at(n, g):
-        return kvt.at[n, :, :, cols(g)]
-
-    sends = []
-
-    def send(cp):
-        cp.start()
-        sends.append(cp)
-
-    for i in zorder:
-        p = (z + i) % Z
-        send(rcopy(snd_g.at[p], seq_at(gseq, 1 + 2 * z + c), s_g.at[i], r_g.at[z], zpeer(p)))
-    for i in zorder:
-        p = (z + i) % Z
-        send(rcopy(snd_q.at[p], qt.at[:, cols(z)], s_q.at[i], r_q.at[z], zpeer(p)))
-    for i in zorder:
-        p = (z + i) % Z
-        n = slot_of[Z - i]
-        send(rcopy(snd_kv.at[p], kv_at(n, gm), s_kv.at[i], r_kv.at[n], zpeer(p)))
-    kvt[0, :, :, cols(gm)] = snd_kv[z]
-    qt[:, cols(z)] = snd_q[z]
-    gseq[(1 + 2 * z + c) // 2, (1 + 2 * z + c) % 2] = snd_g[z]
-
-    def share(n):
-        for i in range(1, 4):
-            rcopy(kv_at(n, gm), kv_at(n, gm), s_grp.at[n, i], r_grp.at[n, gm], gpeer((gm + i) % 4)).start()
-
-    share(0)
-
-    for i in zorder:
-        p = (z + i) % Z
-        rcopy(snd_g.at[p], seq_at(gseq, 1 + 2 * p + c), s_g.at[i], r_g.at[p], zpeer(p)).wait_recv()
+    def live_rows(first, count):
+        frame = first + lax.broadcasted_iota(jnp.int32, (count, 1), 0)
+        return ((frame >= 0) & (frame < length)).astype(F32)
+
+    own_live = live_rows(me * R, R)
+    own = g_in[...].astype(F32) * own_live
+    gx[16 : 16 + R, :] = own
+    snd_g[...] = turned(own)
+    rcopy(g_in.at[pl.ds(R - 16, 16)], gh.at[0], s_h.at[0], r_h.at[0], up).wait_recv()
+    rcopy(g_in.at[pl.ds(0, 16)], gh.at[1], s_h.at[1], r_h.at[1], down).wait_recv()
+    gx[0:16, :] = jnp.where(live_rows(me * R - 16, 16) > 0, gh[0].astype(F32), 0.0)
+    gx[16 + R : 32 + R, :] = jnp.where(live_rows(me * R + R, 16) > 0, gh[1].astype(F32), 0.0)
+
+    def grad_block(b, carry):
+        at = cols(b)
+        total = gx[16 : 16 + R, at]
+        for t in range(T):
+            total = total + ck_in[t : t + 1, at] * gx[pl.ds(16 + HALF - t, R), at]
+        gx2 = (total * own_live).T.astype(BF16)
+        for h in range(R // D):
+            snd_d[(R // D) * b + h] = gx2[h * D : (h + 1) * D]
+        return carry
+
+    lax.fori_loop(0, Z * D // R, grad_block, 0)
+    for i in zorder:
+        p = (z + i) % Z
+        send(rcopy(snd_d.at[p], dot_t.at[:, cols(z)], s_d.at[i], r_d.at[z], zpeer(p)))
+    for i in zorder:
+        p = (z + i) % Z
+        send(rcopy(snd_g.at[p], gbuf.at[z], s_g.at[i], r_g.at[z], zpeer(p)))
+    dot_t[:, cols(z)] = snd_d[z]
+    gbuf[z] = snd_g[z]
 
     def halo(seq, n):
         mine = seq.at[pl.ds(c, Z), 1 - c]
@@ -184,8 +220,6 @@
             cp2.wait_send()
             cp2.wait_recv()
 
-    halo(gseq, 0)
-
     lane = lax.broadcasted_iota(jnp.int32, (1, R), 1)
 
     def live_of(j):
@@ -201,17 +235,6 @@
             return wide[:, R : 2 * R]
         return pltpu.roll(wide, (3 * R - s) % (3 * R), 1)[:, R : 2 * R]
 
-    def grad_block(j, carry):
-        wide, mid = window(gseq, j)
-        total = mid
-        for t in range(T):
-            total = total + kb[t] * shifted(wide, HALF - t)
-        dot_t[:, cols(j)] = (total * live_of(j)).astype(BF16)
-        return carry
-
-    halo_wait(gseq, 0)
-    lax.fori_loop(0, Z, grad_block, 0)
-
     for i in zorder:
         p = (z + i) % Z
         rcopy(snd_q.at[p], qt.at[:, cols(p)], s_q.at[i], r_q.at[p], zpeer(p)).wait_recv()
@@ -223,17 +246,26 @@
     def keys_at(n):
         return pl.ds(pl.multiple_of(n * CK, CK), CK)
 
+    def arrive(n):
+        rcopy(kv_at(n, gm), kv_at(n, gm), s_kv.at[0], r_kv.at[n], gpeer(across)).wait_recv()
+        share(n)
+
+    arrive(1)
+    relay(0)
+
     def forward(n, carry):
         @pl.when(n < Z)
         def _():
-            rcopy(kv_at(n, gm), kv_at(n, gm), s_kv.at[0], r_kv.at[n], gpeer(gm)).wait_recv()
-            share(n)
-
-        m = n - 1
+            arrive(n)
+
+        @pl.when(n <= Z)
+        def _():
+            relay(n - 1)
+
+        m = n - 2
         zs = (z + off_of(m)) % Z
-        for i in range(1, 4):
-            g = (gm + i) % 4
-            rcopy(kv_at(m, g), kv_at(m, g), s_grp.at[m, i], r_grp.at[m, g], gpeer(g)).wait_recv()
+        grp_copy(m, sib, 0, sib).wait_recv()
+        grp_copy(m, across_sib, 2, sib).wait_recv()
         for g in range(4):
             blk = kvt[m, :, :, g * R : (g + 1) * R].reshape(2 * D, R).astype(F32).T
             at = pl.ds(pl.multiple_of(m * CK + g * R, R), R)
@@ -255,7 +287,12 @@
         m_all[m, 0:1, :] = m_new
         return carry
 
-    lax.fori_loop(1, Z + 1, forward, 0)
+    lax.fori_loop(2, Z + 2, forward, 0)
+
+    for i in zorder:
+        p = (z + i) % Z
+        rcopy(snd_d.at[p], dot_t.at[:, cols(p)], s_d.at[i], r_d.at[p], zpeer(p)).wait_recv()
+
 
     inv = 1.0 / l_run[0:1, :]
     l_run[0:1, :] = inv
@@ -268,8 +305,7 @@
 
     def out_block(j, carry):
         wide, mid = window(oseq, j)
-        p = 1 + 2 * j + c
-        grad = gseq[p // 2, p % 2].astype(F32)
+        grad = gbuf[j].astype(F32)
         total = mid
         for t in range(T):
             seg = shifted(wide, t - HALF)
@@ -334,13 +370,16 @@
             part_copy(n, i).start()
         dq_acc[...] = dq_acc[...] + dot(kvt[n, 0], ds)
 
-        @pl.when(k > 0)
-        def _():
-            add_up(n + 1)
-            kv_copy(n + 1, z).start()
+        @pl.when(k > 1)
+        def _():
+            add_up(n + 2)
+            kv_copy(n + 2, z).start()
 
         @pl.when(k == 0)
         def _():
+            for i in zorder:
+                p = (z + i) % Z
+                rcopy(snd_g.at[p], gbuf.at[p], s_g.at[i], r_g.at[p], zpeer(p)).wait_recv()
             halo_wait(oseq, 2)
             lax.fori_loop(0, Z, out_block, 0)
             for i in zorder:
@@ -353,7 +392,7 @@
             for i in range(1, 4):
                 taps_a(i).start()
 
-        @pl.when(k == (Z + 1) // 3)
+        @pl.when(k == min(4, Z - 1))
         def _():
             for i in range(1, 4):
                 taps_a_in(i).wait_recv()
@@ -361,17 +400,6 @@
             for i in range(1, NDP):
                 taps_b(i).start()
 
-        @pl.when(k == Z - 2)
-        def _():
-            for i in range(1, NDP):
-                taps_b_in(i).wait_recv()
-            total = kg_dp[0]
-            for i in range(1, NDP):
-                total = total + kg_dp[i]
-            kg_s[...] = total
-            for i in zorder:
-                taps_c(i, (z + i) % Z, z).start()
-
         return carry
 
     lax.fori_loop(0, Z, backward, 0)
@@ -384,6 +412,16 @@
 
     for i in zorder:
         dq_copy(i, (z + i) % Z, z).start()
+    add_up(1)
+    kv_copy(1, z).start()
+    for i in range(1, NDP):
+        taps_b_in(i).wait_recv()
+    total = kg_dp[0]
+    for i in range(1, NDP):
+        total = total + kg_dp[i]
+    kg_s[...] = total
+    for i in zorder:
+        taps_c(i, (z + i) % Z, z).start()
     add_up(0)
     local = [
         pltpu.make_async_copy(mix_s.at[z], land.at[z, 0], s_loc.at[0]),
@@ -398,8 +436,10 @@
         cp.wait_send()
 
     def drain(n, carry):
+        grp_copy(n, gm, 0, sib).wait_send()
+        grp_copy(n, gm, 1, across).wait_send()
+        grp_copy(n, across, 2, sib).wait_send()
         for i in range(1, 4):
-            rcopy(kv_at(n, gm), kv_at(n, gm), s_grp.at[n, i], r_grp.at[n, gm], gpeer((gm + i) % 4)).wait_send()
             part_copy(n, i).wait_send()
         return carry
 
@@ -437,10 +477,11 @@
     dma = pltpu.SemaphoreType.DMA
     scratch = [
         vm((R, W), BF16), vm((R, W), BF16), vm((R, W), BF16), vm((R, W), BF16), vm((T, W), F32),
-        vm((Z, 2, D, R), BF16), vm((Z, D, R), BF16), vm((Z, D, R), BF16),
+        vm((Z, 2, D, R), BF16), vm((Z, D, R), BF16), vm((Z, D, R), BF16), vm((Z, D, R), BF16),
+        vm((R + 32, W), F32), vm((2, 16, W), BF16), vm((Z, D, R), BF16),
         vm((Z, 2, D, CK), BF16), vm((NK, 2 * D), BF16), vm((NK, 2 * D), BF16),
         vm((D, NQ), BF16), vm((2 * D, NQ), BF16),
-        vm((Z + 1, 2, D, R), BF16), vm((Z + 1, 2, D, R), BF16),
+        vm((Z + 1, 2, D, R), BF16),
         vm((D, NQ), BF16), vm((2 * D, NQ), BF16),
         vm((T, D, R), F32), vm((T, D, R), F32), vm((R, W), F32),
         vm((4, 32, R), F32), vm((NDP, 32, R), F32), vm((32, R), F32), vm((W, R), F32),
@@ -449,7 +490,7 @@
         vm((Z, D, R), BF16), vm((Z, D, R), BF16),
         vm((Z, 2, D, CK), BF16), vm((Z, 4, 2, D, R), BF16), vm((Z, 2, D, R), BF16),
         dma((5,)),
-        dma((Z,)), dma((Z,)), dma((Z,)), dma((Z,)), dma((Z,)), dma((Z,)),
+        dma((Z,)), dma((Z,)), dma((Z,)), dma((Z,)), dma((Z,)), dma((Z,)), dma((Z,)), dma((Z,)),
         dma((Z, 4)), dma((Z, 4)), dma((4,)), dma((4,)),
         dma((4 + NDP + Z,)), dma((4 + NDP + Z,)), dma((Z,)), dma((Z,)), dma((Z,)), dma((Z,)),
         dma((Z, 4)), dma((Z, 4)), dma((Z,)), dma((Z,)), dma((4,)),

time: 74.1 us -> 69.2 us (0.934)
  Pallas kernels: 73.3 us -> 68.4 us
    pallas_call x1, Pallas kernels: 71.4 us -> 66.4 us  [per_device(): pl.pallas_call(functools.partial(kernel, Z, NDP), out_shape=(jax.ShapeDty...]
where the time goes in v3:
time: 69.2 us; the launch traced here: 69.1 us
  Pallas kernels  68.4 us (99%)
    pallas_call x1, Pallas kernels, per_device(): pl.pallas_call(functools.partial(kernel, Z, NDP), out_shape=(jax.ShapeDty...  66.4 us
    pallas_call x1, Pallas kernels, per_device(): pl.pallas_call(functools.partial(finish, Z, T), out_shape=(jax.ShapeDtype...  1.97 us

profile of v3, /device:TPU:1, one launch (start us, length us, event | category | flops | bytes accessed | tf_op | source)
XLA Modules:
  0.0 69.1 jit_solution(8063944867708232592)
XLA Ops:
  0.6 66.4 %shard_map.101 = (bf16[8,4,64,128]{3,2,1,0:T(8,128)(2,1)}, f32[8,32,128]{2,1,0:T(8,128)}) custom-call(s32[8]{0:T(128)} %len_ref.1, bf16[128,512]{1,0:T(8,128)(2,1)} %bitcast.8, bf16[128,512]{1,0:T(8,128)(2,1)} %bitcast.9, bf16[128,512]{1,0:T(8,128)(2,1)} %bitcast.10, bf16[128,512]{1,0:T(8,128)(2,1)} %bitcast.11, f32[31,512]{1,0:T(8,128)} %ck_hbm.1), custom_call_target="tpu_custom_call" | custom-call | flops 3221225472 | bytes 1179648 | tf_op jit(solution)/shard_map/pallas_call | solution.py:500
  67.1 2.0 %shard_map.102 = (bf16[128,512]{1,0:T(8,128)(2,1)}, bf16[128,512]{1,0:T(8,128)(2,1)}, bf16[128,512]{1,0:T(8,128)(2,1)}, bf16[128,512]{1,0:T(8,128)(2,1)}, f32[31,512]{1,0:T(8,128)}) custom-call(bf16[8,4,64,128]{3,2,1,0:T(8,128)(2,1)} %get-tuple-element.12.land, f32[8,32,128]{2,1,0:T(8,128)} %get-tuple-element.13.kg), custom_call_target="tpu_custom_call" | custom-call | tf_op jit(solution)/shard_map/pallas_call | solution.py:516

commit v4 on v3

--- a/solution.py
+++ b/solution.py
@@ -121,13 +121,19 @@
     up, down = (dp, (me + 1) % N), (dp, (me + N - 1) % N)
     send(rcopy(g_in.at[pl.ds(R - 16, 16)], gh.at[0], s_h.at[0], r_h.at[0], up))
     send(rcopy(g_in.at[pl.ds(0, 16)], gh.at[1], s_h.at[1], r_h.at[1], down))
+
+    def send_kv(near):
+        for i in zorder:
+            p = (z + i) % Z
+            n = slot_of[Z - i]
+            if (n < 3) == near:
+                send(rcopy(snd_kv.at[p], kv_at(n, gm), s_kv.at[i], r_kv.at[n], zpeer(p)))
+
+    send_kv(True)
     for i in zorder:
         p = (z + i) % Z
         send(rcopy(snd_q.at[p], qt.at[:, cols(z)], s_q.at[i], r_q.at[z], zpeer(p)))
-    for i in zorder:
-        p = (z + i) % Z
-        n = slot_of[Z - i]
-        send(rcopy(snd_kv.at[p], kv_at(n, gm), s_kv.at[i], r_kv.at[n], zpeer(p)))
+    send_kv(False)
     kvt[0, :, :, cols(gm)] = snd_kv[z]
 
     def grp_copy(n, g, k, to):
@@ -235,6 +241,14 @@
             return wide[:, R : 2 * R]
         return pltpu.roll(wide, (3 * R - s) % (3 * R), 1)[:, R : 2 * R]
 
+    def arrive(n):
+        rcopy(kv_at(n, gm), kv_at(n, gm), s_kv.at[0], r_kv.at[n], gpeer(across)).wait_recv()
+        share(n)
+
+    arrive(1)
+    relay(0)
+    if Z > 2:
+        arrive(2)
     for i in zorder:
         p = (z + i) % Z
         rcopy(snd_q.at[p], qt.at[:, cols(p)], s_q.at[i], r_q.at[p], zpeer(p)).wait_recv()
@@ -246,23 +260,16 @@
     def keys_at(n):
         return pl.ds(pl.multiple_of(n * CK, CK), CK)
 
-    def arrive(n):
-        rcopy(kv_at(n, gm), kv_at(n, gm), s_kv.at[0], r_kv.at[n], gpeer(across)).wait_recv()
-        share(n)
-
-    arrive(1)
-    relay(0)
-
     def forward(n, carry):
         @pl.when(n < Z)
         def _():
             arrive(n)
 
-        @pl.when(n <= Z)
-        def _():
-            relay(n - 1)
-
-        m = n - 2
+        @pl.when(n - 2 < Z)
+        def _():
+            relay(n - 2)
+
+        m = n - 3
         zs = (z + off_of(m)) % Z
         grp_copy(m, sib, 0, sib).wait_recv()
         grp_copy(m, across_sib, 2, sib).wait_recv()
@@ -287,7 +294,7 @@
         m_all[m, 0:1, :] = m_new
         return carry
 
-    lax.fori_loop(2, Z + 2, forward, 0)
+    lax.fori_loop(3, Z + 3, forward, 0)
 
     for i in zorder:
         p = (z + i) % Z
@@ -375,7 +382,7 @@
             add_up(n + 2)
             kv_copy(n + 2, z).start()
 
-        @pl.when(k == 0)
+        @pl.when(k == 1)
         def _():
             for i in zorder:
                 p = (z + i) % Z
@@ -388,7 +395,8 @@
             red = jnp.zeros((D, R), F32)
             for t in range(T):
                 red = jnp.where(lane_d == t, jnp.sum(kga[t], axis=1, keepdims=True), red)
-            kg_grp[gm] = jnp.concatenate([red, jnp.zeros((R - D, R), F32)], axis=0).T[0:32, :]
+            flat = jnp.concatenate([red, jnp.zeros((R - D, R), F32)], axis=0).T
+            kg_grp[gm] = jnp.concatenate([flat[0:16, 0:D], flat[16:32, 0:D]], axis=1)
             for i in range(1, 4):
                 taps_a(i).start()
 
@@ -462,9 +470,11 @@
 def finish(Z, T, land, kg, mix_out, dq_out, dk_out, dv_out, kg_out):
     for n, out in enumerate((mix_out, dq_out, dk_out, dv_out)):
         out[...] = land[:, n].astype(F32).reshape(Z * D, R).T.astype(BF16)
+    def taps_of(h):
+        return jnp.concatenate([kg[h][:, 0:D], kg[h][:, D : 2 * D]], axis=0)[0:T]
+
     for h in range(0, Z, 2):
-        both = jnp.concatenate([kg[h][0:T, 0:D], kg[h + 1][0:T, 0:D]], axis=1)
-        kg_out[:, h * D : (h + 2) * D] = both
+        kg_out[:, h * D : (h + 2) * D] = jnp.concatenate([taps_of(h), taps_of(h + 1)], axis=1)
 
 
 def per_device(Z, NDP, lengths, q, k, v, g, taps):
@@ -484,7 +494,7 @@
         vm((Z + 1, 2, D, R), BF16),
         vm((D, NQ), BF16), vm((2 * D, NQ), BF16),
         vm((T, D, R), F32), vm((T, D, R), F32), vm((R, W), F32),
-        vm((4, 32, R), F32), vm((NDP, 32, R), F32), vm((32, R), F32), vm((W, R), F32),
+        vm((4, 16, R), F32), vm((NDP, 16, R), F32), vm((16, R), F32), vm((W, R), F32),
         vm((NK, NQ), BF16), vm((Z, 8, NQ), F32), vm((8, NQ), F32), vm((8, NQ), F32),
         vm((D, NQ), F32), vm((D, NQ), F32),
         vm((Z, D, R), BF16), vm((Z, D, R), BF16),
@@ -501,7 +511,7 @@
         functools.partial(kernel, Z, NDP),
         out_shape=(
             jax.ShapeDtypeStruct((Z, 4, D, R), BF16),
-            jax.ShapeDtypeStruct((Z, 32, R), F32),
+            jax.ShapeDtypeStruct((Z, 16, R), F32),
         ),
         in_specs=[pl.BlockSpec(memory_space=pltpu.SMEM)] + [anyspec] * 5,
         out_specs=(anyspec, anyspec),

time: 69.2 us -> 62.3 us (0.900)
  Pallas kernels: 68.4 us -> 61.6 us
    pallas_call x1, Pallas kernels: 66.4 us -> 59.6 us  [per_device(): pl.pallas_call(functools.partial(kernel, Z, NDP), out_shape=(jax.ShapeDty...]
where the time goes in v4:
time: 62.3 us; the launch traced here: 62.2 us
  Pallas kernels  61.6 us (99%)
  between operations  0.64 us (1%)
    pallas_call x1, Pallas kernels, per_device(): pl.pallas_call(functools.partial(kernel, Z, NDP), out_shape=(jax.ShapeDty...  59.6 us
    pallas_call x1, Pallas kernels, per_device(): pl.pallas_call(functools.partial(finish, Z, T), out_shape=(jax.ShapeDtype...  1.99 us

profile of v4, /device:TPU:1, one launch (start us, length us, event | category | flops | bytes accessed | tf_op | source)
XLA Modules:
  0.0 62.2 jit_solution(18114777214304399344)
XLA Ops:
  0.6 59.6 %shard_map.101 = (bf16[8,4,64,128]{3,2,1,0:T(8,128)(2,1)}, f32[8,16,128]{2,1,0:T(8,128)}) custom-call(s32[8]{0:T(128)} %len_ref.1, bf16[128,512]{1,0:T(8,128)(2,1)} %bitcast.8, bf16[128,512]{1,0:T(8,128)(2,1)} %bitcast.9, bf16[128,512]{1,0:T(8,128)(2,1)} %bitcast.10, bf16[128,512]{1,0:T(8,128)(2,1)} %bitcast.11, f32[31,512]{1,0:T(8,128)} %ck_hbm.1), custom_call_target="tpu_custom_call" | custom-call | flops 3221225472 | bytes 1179648 | tf_op jit(solution)/shard_map/pallas_call | solution.py:510
  60.2 2.0 %shard_map.102 = (bf16[128,512]{1,0:T(8,128)(2,1)}, bf16[128,512]{1,0:T(8,128)(2,1)}, bf16[128,512]{1,0:T(8,128)(2,1)}, bf16[128,512]{1,0:T(8,128)(2,1)}, f32[31,512]{1,0:T(8,128)}) custom-call(bf16[8,4,64,128]{3,2,1,0:T(8,128)(2,1)} %get-tuple-element.12.land, f32[8,16,128]{2,1,0:T(8,128)} %get-tuple-element.13.kg), custom_call_target="tpu_custom_call" | custom-call | tf_op jit(solution)/shard_map/pallas_call | solution.py:526

commit v5 on v4

--- a/solution.py
+++ b/solution.py
@@ -28,7 +28,7 @@
     land, kg_land,
     q_in, k_in, v_in, g_in, ck_in,
     snd_kv, snd_q, snd_g, snd_d, gx, gh, gbuf, kvt, kvn, kaug, qt, qaug, oseq, dot_t, gfc,
-    kb, kga, kgt, kg_grp, kg_dp, kg_s, kg_s1,
+    kb, kga, kgt, ox, kg_grp, kg_dp, kg_s,
     w_all, m_all, m_run, l_run, acc, dq_acc, mix_s, dq_s, part, gred, kv_s,
     s_in, s_kv, r_kv, s_q, r_q, s_g, r_g, s_d, r_d, s_grp, r_grp, s_h, r_h,
     s_kg, r_kg, s_m, r_m, s_dq, r_dq, s_p, r_p, s_o, r_o, s_loc,
@@ -150,13 +150,10 @@
     share(0)
     qt[:, cols(z)] = snd_q[z]
 
-    kgt[...] = jnp.zeros_like(kgt)
-    kgt[0:T, :] = ck_in[...]
-    for b in range(Z * D // R):
-        kg_s1[b * R : (b + 1) * R, :] = kgt[:, b * R : (b + 1) * R].T
-    my_taps = kg_s1[pl.ds(pl.multiple_of(z * D, D), D), :]
-    for t in range(T):
-        kb[t] = jnp.broadcast_to(my_taps[:, t : t + 1], (D, R))
+    pair = ck_in[:, cols(z // 2)]
+    swapped = pltpu.roll(pair, D, 1)
+    in_low = lax.broadcasted_iota(jnp.int32, (T, R), 1) // D
+    kb[...] = jnp.where(in_low == z % 2, pair, swapped)
     kga[...] = jnp.zeros_like(kga)
     m_run[...] = jnp.full(m_run.shape, FILL, F32)
     l_run[...] = jnp.zeros_like(l_run)
@@ -234,12 +231,7 @@
     def window(seq, j):
         p = 1 + 2 * j + c
         parts = [seq[(p + d) // 2, (p + d) % 2].astype(F32) for d in (-1, 0, 1)]
-        return jnp.concatenate(parts, axis=1), parts[1]
-
-    def shifted(wide, s):
-        if s == 0:
-            return wide[:, R : 2 * R]
-        return pltpu.roll(wide, (3 * R - s) % (3 * R), 1)[:, R : 2 * R]
+        return parts
 
     def arrive(n):
         rcopy(kv_at(n, gm), kv_at(n, gm), s_kv.at[0], r_kv.at[n], gpeer(across)).wait_recv()
@@ -310,15 +302,21 @@
     halo(oseq, 2)
     m_run[1:2, :] = jnp.sum(dot_t[...].astype(F32) * att.astype(F32), axis=0, keepdims=True)
 
+    HZ = Z // 2
+
     def out_block(j, carry):
-        wide, mid = window(oseq, j)
-        grad = gbuf[j].astype(F32)
-        total = mid
+        low, high = window(oseq, j), window(oseq, j + HZ)
+        for n in range(3):
+            ox[n * R : (n + 1) * R, :] = jnp.concatenate([low[n], high[n]], axis=0).T
+        grad = jnp.concatenate([gbuf[j].astype(F32), gbuf[j + HZ].astype(F32)], axis=0).T
+        total = ox[R : 2 * R, :]
         for t in range(T):
-            seg = shifted(wide, t - HALF)
-            total = total + kb[t] * seg
-            kga[t] = kga[t] + grad * seg
-        mix_s[j] = (total * live_of(j)).astype(BF16)
+            seg = ox[pl.ds(R + t - HALF, R), :]
+            total = total + kb[t : t + 1, :] * seg
+            kga[t] = kga[t] + jnp.sum((grad * seg).reshape(R // 8, 8, R), axis=0)
+        mixed = total.T
+        mix_s[j] = (mixed[0:D] * live_of(j)).astype(BF16)
+        mix_s[j + HZ] = (mixed[D : 2 * D] * live_of(j + HZ)).astype(BF16)
         return carry
 
     def mix_copy(i, p, h):
@@ -388,15 +386,16 @@
                 p = (z + i) % Z
                 rcopy(snd_g.at[p], gbuf.at[p], s_g.at[i], r_g.at[p], zpeer(p)).wait_recv()
             halo_wait(oseq, 2)
-            lax.fori_loop(0, Z, out_block, 0)
+            lax.fori_loop(0, HZ, out_block, 0)
             for i in zorder:
                 mix_copy(i, (z + i) % Z, z).start()
-            lane_d = lax.broadcasted_iota(jnp.int32, (D, R), 1)
-            red = jnp.zeros((D, R), F32)
+            kgt[...] = jnp.zeros_like(kgt)
             for t in range(T):
-                red = jnp.where(lane_d == t, jnp.sum(kga[t], axis=1, keepdims=True), red)
-            flat = jnp.concatenate([red, jnp.zeros((R - D, R), F32)], axis=0).T
-            kg_grp[gm] = jnp.concatenate([flat[0:16, 0:D], flat[16:32, 0:D]], axis=1)
+                kgt[t : t + 1, :] = jnp.sum(kga[t], axis=0, keepdims=True)
+            rows = kgt[...]
+            rows = rows + pltpu.roll(rows, D, 1)
+            low_half = lax.broadcasted_iota(jnp.int32, (16, R), 1) < D
+            kg_grp[gm] = jnp.where(low_half, rows[0:16], rows[16:32])
             for i in range(1, 4):
                 taps_a(i).start()
 
@@ -493,8 +492,8 @@
         vm((D, NQ), BF16), vm((2 * D, NQ), BF16),
         vm((Z + 1, 2, D, R), BF16),
         vm((D, NQ), BF16), vm((2 * D, NQ), BF16),
-        vm((T, D, R), F32), vm((T, D, R), F32), vm((R, W), F32),
-        vm((4, 16, R), F32), vm((NDP, 16, R), F32), vm((16, R), F32), vm((W, R), F32),
+        vm((T, R), F32), vm((T, 8, R), F32), vm((32, R), F32), vm((3 * R, R), F32),
+        vm((4, 16, R), F32), vm((NDP, 16, R), F32), vm((16, R), F32),
         vm((NK, NQ), BF16), vm((Z, 8, NQ), F32), vm((8, NQ), F32), vm((8, NQ), F32),
         vm((D, NQ), F32), vm((D, NQ), F32),
         vm((Z, D, R), BF16), vm((Z, D, R), BF16),

time: 62.3 us -> 61.2 us (0.982)
  Pallas kernels: 61.6 us -> 60.4 us
    pallas_call x1, Pallas kernels: 59.6 us -> 58.4 us  [per_device(): pl.pallas_call(functools.partial(kernel, Z, NDP), out_shape=(jax.ShapeDty...]
where the time goes in v5:
time: 61.2 us; the launch traced here: 61.1 us
  Pallas kernels  60.4 us (99%)
  between operations  0.64 us (1%)
    pallas_call x1, Pallas kernels, per_device(): pl.pallas_call(functools.partial(kernel, Z, NDP), out_shape=(jax.ShapeDty...  58.4 us
    pallas_call x1, Pallas kernels, per_device(): pl.pallas_call(functools.partial(finish, Z, T), out_shape=(jax.ShapeDtype...  1.99 us

profile of v5, /device:TPU:1, one launch (start us, length us, event | category | flops | bytes accessed | tf_op | source)
XLA Modules:
  0.0 61.1 jit_solution(3796524020668458706)
XLA Ops:
  0.6 58.4 %shard_map.101 = (bf16[8,4,64,128]{3,2,1,0:T(8,128)(2,1)}, f32[8,16,128]{2,1,0:T(8,128)}) custom-call(s32[8]{0:T(128)} %len_ref.1, bf16[128,512]{1,0:T(8,128)(2,1)} %bitcast.8, bf16[128,512]{1,0:T(8,128)(2,1)} %bitcast.9, bf16[128,512]{1,0:T(8,128)(2,1)} %bitcast.10, bf16[128,512]{1,0:T(8,128)(2,1)} %bitcast.11, f32[31,512]{1,0:T(8,128)} %ck_hbm.1), custom_call_target="tpu_custom_call" | custom-call | flops 3221225472 | bytes 1179648 | tf_op jit(solution)/shard_map/pallas_call | solution.py:509
  59.1 2.0 %shard_map.102 = (bf16[128,512]{1,0:T(8,128)(2,1)}, bf16[128,512]{1,0:T(8,128)(2,1)}, bf16[128,512]{1,0:T(8,128)(2,1)}, bf16[128,512]{1,0:T(8,128)(2,1)}, f32[31,512]{1,0:T(8,128)}) custom-call(bf16[8,4,64,128]{3,2,1,0:T(8,128)(2,1)} %get-tuple-element.12.land, f32[8,16,128]{2,1,0:T(8,128)} %get-tuple-element.13.kg), custom_call_target="tpu_custom_call" | custom-call | tf_op jit(solution)/shard_map/pallas_call | solution.py:525

commit v6 on v5

--- a/solution.py
+++ b/solution.py
@@ -252,6 +252,8 @@
     def keys_at(n):
         return pl.ds(pl.multiple_of(n * CK, CK), CK)
 
+    ones = jnp.ones((16, CK), BF16)
+
     def forward(n, carry):
         @pl.when(n < Z)
         def _():
@@ -278,10 +280,9 @@
         m_new = jnp.maximum(m_old, jnp.max(s, axis=0, keepdims=True))
         w = jnp.exp(s - m_new)
         alpha = jnp.exp(m_old - m_new)
-        l_run[0:1, :] = l_run[0:1, :] * alpha + jnp.sum(w, axis=0, keepdims=True)
         wb = w.astype(BF16)
         w_all[at, :] = wb
-        acc[...] = acc[...] * alpha + dot(kvt[m, 1], wb)
+        acc[...] = acc[...] * alpha + dot(jnp.concatenate([kvt[m, 1], ones], axis=0), wb)
         m_run[0:1, :] = m_new
         m_all[m, 0:1, :] = m_new
         return carry
@@ -293,9 +294,9 @@
         rcopy(snd_d.at[p], dot_t.at[:, cols(p)], s_d.at[i], r_d.at[p], zpeer(p)).wait_recv()
 
 
-    inv = 1.0 / l_run[0:1, :]
+    inv = 1.0 / acc[D : D + 1, :]
     l_run[0:1, :] = inv
-    att = (acc[...] * inv).astype(BF16)
+    att = (acc[0:D, :] * inv).astype(BF16)
     for j in range(Z):
         blk = (att[:, j * R : (j + 1) * R].astype(F32) * live_of(j)).astype(BF16)
         oseq[(1 + 2 * j + c) // 2, (1 + 2 * j + c) % 2] = blk
@@ -360,6 +361,9 @@
     def kv_copy(n, h):
         return rcopy(kv_s.at[n], land.at[h, pl.ds(2, 2)], s_o.at[n], r_o.at[h], zpeer((z + off_of(n)) % Z))
 
+    def dq_copy(i, p, h):
+        return rcopy(dq_s.at[p], land.at[h, 1], s_dq.at[i], r_dq.at[h], zpeer(p))
+
     def backward(k, carry):
         n = Z - 1 - k
         at = keys_at(n)
@@ -369,18 +373,26 @@
         dp_t = dot(kvn[at, :], gfc[...])
         wb = w_all[at, :]
         ds = (wb.astype(F32) * (dp_t - m_run[1:2, :] * f)).astype(BF16)
+        dq_acc[...] = dq_acc[...] + dot(kvt[n, 0], ds)
+
+        @pl.when(k == Z - 1)
+        def _():
+            for j in range(Z):
+                dq_s[j] = (dq_acc[:, j * R : (j + 1) * R] * (D ** -0.5)).astype(BF16)
+            for i in zorder:
+                dq_copy(i, (z + i) % Z, z).start()
+
         part[n, 0] = (dot(qt[...], ds, NT) * (D ** -0.5)).astype(BF16)
         part[n, 1] = dot(gf, wb, NT).astype(BF16)
         for i in range(1, 4):
             part_copy(n, i).start()
-        dq_acc[...] = dq_acc[...] + dot(kvt[n, 0], ds)
 
         @pl.when(k > 1)
         def _():
             add_up(n + 2)
             kv_copy(n + 2, z).start()
 
-        @pl.when(k == 1)
+        @pl.when(k == 0)
         def _():
             for i in zorder:
                 p = (z + i) % Z
@@ -399,7 +411,7 @@
             for i in range(1, 4):
                 taps_a(i).start()
 
-        @pl.when(k == min(4, Z - 1))
+        @pl.when(k == min(2, Z - 1))
         def _():
             for i in range(1, 4):
                 taps_a_in(i).wait_recv()
@@ -407,28 +419,24 @@
             for i in range(1, NDP):
                 taps_b(i).start()
 
+        @pl.when(k == Z - 1)
+        def _():
+            for i in range(1, NDP):
+                taps_b_in(i).wait_recv()
+            total = kg_dp[0]
+            for i in range(1, NDP):
+                total = total + kg_dp[i]
+            kg_s[...] = total.astype(BF16)
+            for i in zorder:
+                taps_c(i, (z + i) % Z, z).start()
+
         return carry
 
     lax.fori_loop(0, Z, backward, 0)
 
-    for j in range(Z):
-        dq_s[j] = (dq_acc[:, j * R : (j + 1) * R] * (D ** -0.5)).astype(BF16)
-
-    def dq_copy(i, p, h):
-        return rcopy(dq_s.at[p], land.at[h, 1], s_dq.at[i], r_dq.at[h], zpeer(p))
-
-    for i in zorder:
-        dq_copy(i, (z + i) % Z, z).start()
+
     add_up(1)
     kv_copy(1, z).start()
-    for i in range(1, NDP):
-        taps_b_in(i).wait_recv()
-    total = kg_dp[0]
-    for i in range(1, NDP):
-        total = total + kg_dp[i]
-    kg_s[...] = total
-    for i in zorder:
-        taps_c(i, (z + i) % Z, z).start()
     add_up(0)
     local = [
         pltpu.make_async_copy(mix_s.at[z], land.at[z, 0], s_loc.at[0]),
@@ -470,7 +478,8 @@
     for n, out in enumerate((mix_out, dq_out, dk_out, dv_out)):
         out[...] = land[:, n].astype(F32).reshape(Z * D, R).T.astype(BF16)
     def taps_of(h):
-        return jnp.concatenate([kg[h][:, 0:D], kg[h][:, D : 2 * D]], axis=0)[0:T]
+        both = kg[h].astype(F32)
+        return jnp.concatenate([both[:, 0:D], both[:, D : 2 * D]], axis=0)[0:T]
 
     for h in range(0, Z, 2):
         kg_out[:, h * D : (h + 2) * D] = jnp.concatenate([taps_of(h), taps_of(h + 1)], axis=1)
@@ -493,9 +502,9 @@
         vm((Z + 1, 2, D, R), BF16),
         vm((D, NQ), BF16), vm((2 * D, NQ), BF16),
         vm((T, R), F32), vm((T, 8, R), F32), vm((32, R), F32), vm((3 * R, R), F32),
-        vm((4, 16, R), F32), vm((NDP, 16, R), F32), vm((16, R), F32),
+        vm((4, 16, R), F32), vm((NDP, 16, R), F32), vm((16, R), BF16),
         vm((NK, NQ), BF16), vm((Z, 8, NQ), F32), vm((8, NQ), F32), vm((8, NQ), F32),
-        vm((D, NQ), F32), vm((D, NQ), F32),
+        vm((D + 16, NQ), F32), vm((D, NQ), F32),
         vm((Z, D, R), BF16), vm((Z, D, R), BF16),
         vm((Z, 2, D, CK), BF16), vm((Z, 4, 2, D, R), BF16), vm((Z, 2, D, R), BF16),
         dma((5,)),
@@ -510,7 +519,7 @@
         functools.partial(kernel, Z, NDP),
         out_shape=(
             jax.ShapeDtypeStruct((Z, 4, D, R), BF16),
-            jax.ShapeDtypeStruct((Z, 16, R), F32),
+            jax.ShapeDtypeStruct((Z, 16, R), BF16),
         ),
         in_specs=[pl.BlockSpec(memory_space=pltpu.SMEM)] + [anyspec] * 5,
         out_specs=(anyspec, anyspec),

time: 61.2 us -> 60 us (0.980)
  Pallas kernels: 60.4 us -> 59.2 us
    pallas_call x1, Pallas kernels: 58.4 us -> 57.2 us  [per_device(): pl.pallas_call(functools.partial(kernel, Z, NDP), out_shape=(jax.ShapeDty...]
where the time goes in v6:
time: 60 us; the launch traced here: 59.8 us
  Pallas kernels  59.2 us (99%)
  between operations  0.64 us (1%)
    pallas_call x1, Pallas kernels, per_device(): pl.pallas_call(functools.partial(kernel, Z, NDP), out_shape=(jax.ShapeDty...  57.2 us
    pallas_call x1, Pallas kernels, per_device(): pl.pallas_call(functools.partial(finish, Z, T), out_shape=(jax.ShapeDtype...  1.98 us

profile of v6, /device:TPU:1, one launch (start us, length us, event | category | flops | bytes accessed | tf_op | source)
XLA Modules:
  0.0 59.8 jit_solution(3900274622112009596)
XLA Ops:
  0.6 57.2 %shard_map.101 = (bf16[8,4,64,128]{3,2,1,0:T(8,128)(2,1)}, bf16[8,16,128]{2,1,0:T(8,128)(2,1)}) custom-call(s32[8]{0:T(128)} %len_ref.1, bf16[128,512]{1,0:T(8,128)(2,1)} %bitcast.8, bf16[128,512]{1,0:T(8,128)(2,1)} %bitcast.9, bf16[128,512]{1,0:T(8,128)(2,1)} %bitcast.10, bf16[128,512]{1,0:T(8,128)(2,1)} %bitcast.11, f32[31,512]{1,0:T(8,128)} %ck_hbm.1), custom_call_target="tpu_custom_call" | custom-call | flops 3221225472 | bytes 1179648 | tf_op jit(solution)/shard_map/pallas_call | solution.py:518
  57.9 2.0 %shard_map.102 = (bf16[128,512]{1,0:T(8,128)(2,1)}, bf16[128,512]{1,0:T(8,128)(2,1)}, bf16[128,512]{1,0:T(8,128)(2,1)}, bf16[128,512]{1,0:T(8,128)(2,1)}, f32[31,512]{1,0:T(8,128)}) custom-call(bf16[8,4,64,128]{3,2,1,0:T(8,128)(2,1)} %get-tuple-element.12.land, bf16[8,16,128]{2,1,0:T(8,128)(2,1)} %get-tuple-element.13.kg), custom_call_target="tpu_custom_call" | custom-call | tf_op jit(solution)/shard_map/pallas_call | solution.py:534

commit v7 on v6

--- a/solution.py
+++ b/solution.py
@@ -392,7 +392,7 @@
             add_up(n + 2)
             kv_copy(n + 2, z).start()
 
-        @pl.when(k == 0)
+        @pl.when(k == 1)
         def _():
             for i in zorder:
                 p = (z + i) % Z
@@ -411,7 +411,7 @@
             for i in range(1, 4):
                 taps_a(i).start()
 
-        @pl.when(k == min(2, Z - 1))
+        @pl.when(k == min(3, Z - 1))
         def _():
             for i in range(1, 4):
                 taps_a_in(i).wait_recv()

time: 60 us -> 58.5 us (0.975)
  Pallas kernels: 59.2 us -> 57.7 us
    pallas_call x1, Pallas kernels: 57.2 us -> 55.7 us  [per_device(): pl.pallas_call(functools.partial(kernel, Z, NDP), out_shape=(jax.ShapeDty...]
where the time goes in v7:
time: 58.5 us; the launch traced here: 58.3 us
  Pallas kernels  57.7 us (99%)
  between operations  0.64 us (1%)
    pallas_call x1, Pallas kernels, per_device(): pl.pallas_call(functools.partial(kernel, Z, NDP), out_shape=(jax.ShapeDty...  55.7 us
    pallas_call x1, Pallas kernels, per_device(): pl.pallas_call(functools.partial(finish, Z, T), out_shape=(jax.ShapeDtype...  1.98 us

profile of v7, /device:TPU:1, one launch (start us, length us, event | category | flops | bytes accessed | tf_op | source)
XLA Modules:
  0.0 58.3 jit_solution(15466725815333337191)
XLA Ops:
  0.6 55.7 %shard_map.101 = (bf16[8,4,64,128]{3,2,1,0:T(8,128)(2,1)}, bf16[8,16,128]{2,1,0:T(8,128)(2,1)}) custom-call(s32[8]{0:T(128)} %len_ref.1, bf16[128,512]{1,0:T(8,128)(2,1)} %bitcast.8, bf16[128,512]{1,0:T(8,128)(2,1)} %bitcast.9, bf16[128,512]{1,0:T(8,128)(2,1)} %bitcast.10, bf16[128,512]{1,0:T(8,128)(2,1)} %bitcast.11, f32[31,512]{1,0:T(8,128)} %ck_hbm.1), custom_call_target="tpu_custom_call" | custom-call | flops 3221225472 | bytes 1179648 | tf_op jit(solution)/shard_map/pallas_call | solution.py:518
  56.3 2.0 %shard_map.102 = (bf16[128,512]{1,0:T(8,128)(2,1)}, bf16[128,512]{1,0:T(8,128)(2,1)}, bf16[128,512]{1,0:T(8,128)(2,1)}, bf16[128,512]{1,0:T(8,128)(2,1)}, f32[31,512]{1,0:T(8,128)}) custom-call(bf16[8,4,64,128]{3,2,1,0:T(8,128)(2,1)} %get-tuple-element.12.land, bf16[8,16,128]{2,1,0:T(8,128)(2,1)} %get-tuple-element.13.kg), custom_call_target="tpu_custom_call" | custom-call | tf_op jit(solution)/shard_map/pallas_call | solution.py:534
